TPU v7x, 512 devices: a whole 4x4x16 slice. The times are simulated.
512 devices in a mesh: lon: 32 (over y_lo, z), lat: 16 (over x, y_hi, core).
Axes of the slice: x: 4, y: 4 (y_hi: 2, y_lo: 2; y = y_hi * 2 + y_lo), z: 16, core: 2. Of those that a mesh axis runs over, the one named last changes fastest.
Arguments:
- grid_in: bfloat16 [128, 1024, 256], P('lat', 'lon'), may hold values from -6 to 6
- basis: bfloat16 [128, 3, 17, 4], replicated, may hold values from -3 to 3
- widths: int32 [128], replicated, may hold values from 1 to 8, as said below
- weight_one: bfloat16 [4, 256, 256], replicated, may hold values from -0.1875 to 0.1875
- weight_two: bfloat16 [4, 256, 256], replicated, may hold values from -0.1875 to 0.1875
- cotangent: bfloat16 [128, 1024, 256], P('lat', 'lon'), may hold values from -6 to 6
Outputs:
- grad_input: float32 [128, 1024, 256], P('lat', 'lon')
- grad_one: float32 [4, 256, 256], replicated
- grad_two: float32 [4, 256, 256], replicated
Inputs may be any that keep to these rules, and one draw needn't show every extreme that they name: `widths`: both pole rows (row 0 and row 127) have width 8.
All inputs are finite; a program needn't handle non-finite values.
Results may differ from a plain program's by a relative error of at most 0.0067.
Values may be sent and summed in bfloat16 or wider, within the bound.
A program may use at most 64 MiB of HBM per device.

v0:
```python
import jax
import jax.numpy as jnp
from jax import lax
from jax.sharding import PartitionSpec as P

GELU_C = 0.7978845608028654
CUBIC = 0.044715


def extended_2(array, sides, width, wrap):
    for axis, dim in sides:
        count, length = (lax.axis_size(axis), array.shape[dim])
        up = [(i, (i + 1) % count) for i in range(count if wrap else count - 1)]
        down = [(j, i) for i, j in up]
        last = lax.slice_in_dim(array, length - width, length, axis=dim)
        leading = lax.slice_in_dim(array, 0, width, axis=dim)
        before = lax.ppermute(last, axis, up)
        after = lax.ppermute(leading, axis, down)
        array = jnp.concatenate([before, array, after], axis=dim)
    return array


def from_partner(block, axis, stride):
    count = lax.axis_size(axis)
    route = []
    for low in range(count):
        high = low | 1 << stride
        if high != low and high < count:
            route += [(low, high), (high, low)]
    return lax.ppermute(block, axis, route)


def gelu_value(pre_act):
    return (
        0.5 * pre_act * (1.0 + jnp.tanh(GELU_C * (pre_act + CUBIC * pre_act * pre_act * pre_act)))
    )


def gelu_slope(pre_act):
    tanh_val = jnp.tanh(GELU_C * (pre_act + CUBIC * pre_act * pre_act * pre_act))
    return 0.5 * (1.0 + tanh_val) + 0.5 * pre_act * (1.0 - tanh_val * tanh_val) * GELU_C * (
        1.0 + 3.0 * CUBIC * pre_act * pre_act
    )


def masked_basis(basis, widths):
    span_size = basis.shape[2]
    reach_cols = (span_size - 1) // 2
    offsets = jnp.arange(span_size, dtype=jnp.int32) - reach_cols
    keep_mask = (jnp.abs(offsets)[None, :] <= widths[:, None]).astype(jnp.float32)
    return basis.astype(jnp.float32) * keep_mask[:, None, :, None]


def pole_basis(masked):
    blank_slot = jnp.zeros_like(masked[0, 0])
    north_row = jnp.stack([blank_slot, blank_slot, masked[0, 0]])
    south_row = jnp.stack([masked[-1, 2], blank_slot, blank_slot])
    return jnp.concatenate([north_row[None], masked, south_row[None]], axis=0)


def offset_table(col_count, span_size, flipped):
    col_out = jnp.arange(col_count, dtype=jnp.int32)[:, None, None]
    col_in = jnp.arange(col_count + span_size - 1, dtype=jnp.int32)[None, :, None]
    offset_idx = jnp.arange(span_size, dtype=jnp.int32)[None, None, :]
    if flipped:
        diff_index = col_out - col_in + span_size - 1
    else:
        diff_index = col_in - col_out
    return (diff_index == offset_idx).astype(jnp.float32)


def local(grid_in, basis, widths, weight_one, weight_two, cotangent):
    row_count, col_count, chan_count = grid_in.shape
    span_size = basis.shape[2]
    basis_count = basis.shape[3]
    reach_cols = (span_size - 1) // 2
    lat_pos = lax.axis_index("lat")
    lat_count = lax.axis_size("lat")
    half_bit = lax.axis_size("lon").bit_length() - 2
    masked = masked_basis(basis, widths)
    first_row_index = lat_pos * row_count
    own_basis = lax.dynamic_slice_in_dim(masked, first_row_index, row_count, 0)
    forward_band = jnp.einsum(
        "irtk,jmt->irkjm", own_basis, offset_table(col_count, span_size, False)
    ).astype(jnp.bfloat16)

    def extend(values):
        rimmed = extended_2(values, (("lat", 0),), 1, False)
        edge_row = jnp.where(lat_pos == 0, values[0], values[-1])
        turned = from_partner(edge_row, "lon", half_bit)
        top_row = jnp.where(lat_pos == 0, turned, rimmed[0])
        bottom = jnp.where(lat_pos == lat_count - 1, turned, rimmed[-1])
        complete = jnp.concatenate([top_row[None], rimmed[1 : row_count + 1], bottom[None]], axis=0)
        return extended_2(complete, (("lon", 1),), reach_cols, True)

    def convolve(values):
        extended = extend(values)
        stacked = jnp.stack(
            [extended[0:row_count], extended[1 : row_count + 1], extended[2 : row_count + 2]],
            axis=1,
        )
        return jnp.einsum(
            "irkjm,irmc->ijkc", forward_band, stacked, preferred_element_type=jnp.float32
        ).astype(jnp.bfloat16)

    def band_adjoint(extended):
        pole_ext = pole_basis(masked)
        near_basis = lax.dynamic_slice_in_dim(pole_ext, first_row_index, row_count + 2, 0)
        chosen = jnp.stack(
            [
                near_basis[2 : row_count + 2, 0],
                near_basis[1 : row_count + 1, 1],
                near_basis[0:row_count, 2],
            ],
            axis=1,
        )
        adjoint_band = jnp.einsum(
            "irtk,jmt->irkjm", chosen, offset_table(col_count, span_size, True)
        ).astype(jnp.bfloat16)
        stacked = jnp.stack(
            [extended[2 : row_count + 2], extended[1 : row_count + 1], extended[0:row_count]],
            axis=1,
        )
        return jnp.einsum(
            "prkjm,prmkc->pjc", adjoint_band, stacked, preferred_element_type=jnp.float32
        )

    def adjoint(narrow, weight):
        grad_cells = jnp.einsum(
            "ijo,kco->ijkc", narrow, weight, preferred_element_type=jnp.float32
        ).astype(jnp.bfloat16)
        flat_cells = grad_cells.reshape(row_count, col_count, basis_count * chan_count)
        extended = extend(flat_cells).reshape(
            row_count + 2, col_count + 2 * reach_cols, basis_count, chan_count
        )
        return band_adjoint(extended)

    z_one = convolve(grid_in)
    activation = jnp.einsum("ijkc,kco->ijo", z_one, weight_one, preferred_element_type=jnp.float32)
    hidden = gelu_value(activation).astype(jnp.bfloat16)
    z_two = convolve(hidden)
    part_two = jnp.einsum("ijkc,ijo->kco", z_two, cotangent, preferred_element_type=jnp.float32)
    grad_two = lax.psum(part_two, ("lon", "lat"))
    grad_hidden = adjoint(cotangent, weight_two)
    grad_act = (grad_hidden * gelu_slope(activation)).astype(jnp.bfloat16)
    part_one = jnp.einsum("ijkc,ijo->kco", z_one, grad_act, preferred_element_type=jnp.float32)
    grad_input = adjoint(grad_act, weight_one)
    grad_one = lax.psum(part_one, ("lon", "lat"))
    return (grad_input, grad_one, grad_two)


def solution(mesh):
    placed = (P("lat", "lon", None), P(), P(), P(), P(), P("lat", "lon", None))
    return jax.shard_map(
        local,
        mesh=mesh,
        in_specs=placed,
        out_specs=(P("lat", "lon", None), P(), P()),
        check_vma=False,
    )
```

profile of v0, /device:TPU:1, one launch (start us, length us, event | category | flops | bytes accessed | tf_op | source)
XLA Modules:
  0.0 581.1 jit_solution(17400161504375850038)
XLA Ops:
  8.9 4.0 collective-permute-start
  12.9 5.4 collective-permute-start.1
  20.3 2.7 collective-permute-start.6
  22.9 3.2 collective-permute-start.7
  27.2 1.9 collective-permute-start.2
  29.5 11.6 %collective-permute-start.9 = (bf16[10,8,256]{2,1,0:T(8,128)(2,1)S(1)}, bf16[10,8,256]{2,1,0:T(8,128)(2,1)S(1)}, u32[]{:S(2)}, u32[]{:S(2)}) collective-permute-start(bf16[10,8,256]{2,1,0:T(8,128)(2,1)S(1)} %get-tuple-element.32), channel_id=1, source_target_pairs={{16,0},{32,16},{48,32},{64,48},{80,64},{96,80},{112,96},{128,112},... | collective-permute-start | bytes 122888 | tf_op jit(solution)/shard_map/ppermute | solution.py:18
  44.3 3.6 collective-permute-done.8
  49.5 2.6 collective-permute-start.15
  52.1 5.4 collective-permute-start.16
  57.5 1.9 collective-permute-start.17
  59.5 4.6 collective-permute-done.17
  64.1 1.9 collective-permute-start.19
  66.1 3.4 collective-permute-start.18
  69.5 4.2 collective-permute-start.4
  77.3 4.5 collective-permute-done.3
  83.6 2.2 copy.93
  90.5 3.0 collective-permute-start.10
  93.5 4.5 collective-permute-start.11
  101.4 3.7 collective-permute-done.12
  107.1 3.4 collective-permute-start.13
  111.5 3.7 collective-permute-done.13
  117.1 2.1 copy.104
  124.0 446.8 %all-reduce.5.cloned.1.call-done = (f32[4,256,256]{2,1,0:T(8,128)}, f32[4,256,256]{2,1,0:T(8,128)}) async-done(((f32[4,256,256]{2,1,0:T(8,128)}, f32[4,256,256]{2,1,0:T(8,128)}), (f32[4,256,256]{2,1,0:T(8,128)}, f32[4,256,256]{2,1,0:T(8,128)})) %all-reduce.5.cloned.1.call-update) | async-done | bytes 2097168 | tf_op jit(solution)/shard_map/psum | solution.py:148
  570.9 2.4 copy.145
  (115 shorter events, 33.7 us)
Async XLA Ops:
  7.2 41.3 %copy-start = (bf16[4,256,256]{2,1,0:T(8,128)(2,1)S(1)}, bf16[4,256,256]{2,1,0:T(8,128)(2,1)}, u32[]{:S(2)}) copy-start(bf16[4,256,256]{2,1,0:T(8,128)(2,1)} %param.9) | copy-start | bytes 1572868
  7.2 19.0 %copy-start.10 = (bf16[128,3,17,4]{0,3,2,1:T(4,128)(2,1)S(1)}, bf16[128,3,17,4]{0,3,2,1:T(4,128)(2,1)}, u32[]{:S(2)}) copy-start(bf16[128,3,17,4]{0,3,2,1:T(4,128)(2,1)} %param.7) | copy-start | bytes 156676
  7.2 563.7 %all-reduce.5.cloned.1.call-start = ((), (), s32[]{:S(2)}) async-start(), calls=%async_computation | async-start | bytes 4194304 | tf_op jit(solution)/shard_map/psum | solution.py:148
  8.8 17.7 %copy-start.11 = (s32[128]{0:T(128)S(1)}, s32[128]{0:T(128)}, u32[]{:S(2)}) copy-start(s32[128]{0:T(128)} %param.8) | copy-start | bytes 1540
  8.9 48.6 %collective-permute-start = (bf16[32,1024]{1,0:T(8,128)(2,1)S(1)}, bf16[32,1024]{1,0:T(8,128)(2,1)S(1)}, u32[]{:S(2)}, u32[]{:S(2)}) collective-permute-start(bf16[32,1024]{1,0:T(8,128)(2,1)S(1)} %bitcast.201), channel_id=1, source_target_pairs={{0,256},{256,0},{16,272},{272,16},{32,288},{288,32},{48,304},{304,... | collective-permute-start | bytes 196616 | tf_op jit(solution)/shard_map/ppermute | solution.py:30
  12.9 46.5 %collective-permute-start.1 = (bf16[1,32,1024]{2,1,0:T(8,128)(2,1)S(1)}, bf16[1,32,1024]{2,1,0:T(8,128)(2,1)S(1)}, u32[]{:S(2)}, u32[]{:S(2)}) collective-permute-start(bf16[1,32,1024]{2,1,0:T(8,128)(2,1)S(1)} %bitcast.200), channel_id=1, source_target_pairs={{0,1},{1,2},{2,3},{3,4},{4,5},{5,6},{6,7},{7,8},{8,9},{9,10},{10,1... | collective-permute-start | bytes 196616 | tf_op jit(solution)/shard_map/ppermute | solution.py:17
  18.3 8.9 %collective-permute-start.5 = (bf16[32,256]{1,0:T(8,128)(2,1)S(1)}, bf16[32,256]{1,0:T(8,128)(2,1)S(1)}, u32[]{:S(2)}, u32[]{:S(2)}) collective-permute-start(bf16[32,256]{1,0:T(8,128)(2,1)S(1)} %get-tuple-element.37), channel_id=1, source_target_pairs={{0,256},{256,0},{16,272},{272,16},{32,288},{288,32},{48,304},{304,... | collective-permute-start | bytes 49160 | tf_op jit(solution)/shard_map/ppermute | solution.py:30
  20.3 8.9 %collective-permute-start.6 = (bf16[1,32,256]{2,1,0:T(8,128)(2,1)S(1)}, bf16[1,32,256]{2,1,0:T(8,128)(2,1)S(1)}, u32[]{:S(2)}, u32[]{:S(2)}) collective-permute-start(bf16[1,32,256]{2,1,0:T(8,128)(2,1)S(1)} %get-tuple-element.36), channel_id=1, source_target_pairs={{0,1},{1,2},{2,3},{3,4},{4,5},{5,6},{6,7},{7,8},{8,9},{9,10},{10,1... | collective-permute-start | bytes 49160 | tf_op jit(solution)/shard_map/ppermute | solution.py:17
  22.9 6.6 %collective-permute-start.7 = (bf16[1,32,256]{2,1,0:T(8,128)(2,1)S(1)}, bf16[1,32,256]{2,1,0:T(8,128)(2,1)S(1)}, u32[]{:S(2)}, u32[]{:S(2)}) collective-permute-start(bf16[1,32,256]{2,1,0:T(8,128)(2,1)S(1)} %get-tuple-element.38), channel_id=1, source_target_pairs={{1,0},{2,1},{3,2},{4,3},{5,4},{6,5},{7,6},{8,7},{9,8},{10,9},{11,1... | collective-permute-start | bytes 49160 | tf_op jit(solution)/shard_map/ppermute | solution.py:18
  27.2 32.2 %collective-permute-start.2 = (bf16[1,32,1024]{2,1,0:T(8,128)(2,1)S(1)}, bf16[1,32,1024]{2,1,0:T(8,128)(2,1)S(1)}, u32[]{:S(2)}, u32[]{:S(2)}) collective-permute-start(bf16[1,32,1024]{2,1,0:T(8,128)(2,1)S(1)} %bitcast.202), channel_id=1, source_target_pairs={{1,0},{2,1},{3,2},{4,3},{5,4},{6,5},{7,6},{8,7},{9,8},{10,9},{11,1... | collective-permute-start | bytes 196616 | tf_op jit(solution)/shard_map/ppermute | solution.py:18
  29.5 14.8 %collective-permute-start.9 = (bf16[10,8,256]{2,1,0:T(8,128)(2,1)S(1)}, bf16[10,8,256]{2,1,0:T(8,128)(2,1)S(1)}, u32[]{:S(2)}, u32[]{:S(2)}) collective-permute-start(bf16[10,8,256]{2,1,0:T(8,128)(2,1)S(1)} %get-tuple-element.32), channel_id=1, source_target_pairs={{16,0},{32,16},{48,32},{64,48},{80,64},{96,80},{112,96},{128,112},... | collective-permute-start | bytes 122888 | tf_op jit(solution)/shard_map/ppermute | solution.py:18
  41.1 6.9 %collective-permute-start.8 = (bf16[10,8,256]{2,1,0:T(8,128)(2,1)S(1)}, bf16[10,8,256]{2,1,0:T(8,128)(2,1)S(1)}, u32[]{:S(2)}, u32[]{:S(2)}) collective-permute-start(bf16[10,8,256]{2,1,0:T(8,128)(2,1)S(1)} %get-tuple-element.31), channel_id=1, source_target_pairs={{0,16},{16,32},{32,48},{48,64},{64,80},{80,96},{96,112},{112,128},... | collective-permute-start | bytes 122888 | tf_op jit(solution)/shard_map/ppermute | solution.py:17
  49.5 10.1 %collective-permute-start.15 = (bf16[32,256]{1,0:T(8,128)(2,1)S(1)}, bf16[32,256]{1,0:T(8,128)(2,1)S(1)}, u32[]{:S(2)}, u32[]{:S(2)}) collective-permute-start(bf16[32,256]{1,0:T(8,128)(2,1)S(1)} %get-tuple-element.34), channel_id=1, source_target_pairs={{0,256},{256,0},{16,272},{272,16},{32,288},{288,32},{48,304},{304,... | collective-permute-start | bytes 49160 | tf_op jit(solution)/shard_map/ppermute | solution.py:30
  52.1 7.4 %collective-permute-start.16 = (bf16[1,32,256]{2,1,0:T(8,128)(2,1)S(1)}, bf16[1,32,256]{2,1,0:T(8,128)(2,1)S(1)}, u32[]{:S(2)}, u32[]{:S(2)}) collective-permute-start(bf16[1,32,256]{2,1,0:T(8,128)(2,1)S(1)} %get-tuple-element.33), channel_id=1, source_target_pairs={{0,1},{1,2},{2,3},{3,4},{4,5},{5,6},{6,7},{7,8},{8,9},{9,10},{10,1... | collective-permute-start | bytes 49160 | tf_op jit(solution)/shard_map/ppermute | solution.py:17
  57.5 6.6 %collective-permute-start.17 = (bf16[1,32,256]{2,1,0:T(8,128)(2,1)S(1)}, bf16[1,32,256]{2,1,0:T(8,128)(2,1)S(1)}, u32[]{:S(2)}, u32[]{:S(2)}) collective-permute-start(bf16[1,32,256]{2,1,0:T(8,128)(2,1)S(1)} %get-tuple-element.35), channel_id=1, source_target_pairs={{1,0},{2,1},{3,2},{4,3},{5,4},{6,5},{7,6},{8,7},{9,8},{10,9},{11,1... | collective-permute-start | bytes 49160 | tf_op jit(solution)/shard_map/ppermute | solution.py:18
  64.1 11.4 %collective-permute-start.19 = (bf16[10,8,256]{2,1,0:T(8,128)(2,1)S(1)}, bf16[10,8,256]{2,1,0:T(8,128)(2,1)S(1)}, u32[]{:S(2)}, u32[]{:S(2)}) collective-permute-start(bf16[10,8,256]{2,1,0:T(8,128)(2,1)S(1)} %get-tuple-element.30), channel_id=1, source_target_pairs={{16,0},{32,16},{48,32},{64,48},{80,64},{96,80},{112,96},{128,112},... | collective-permute-start | bytes 122888 | tf_op jit(solution)/shard_map/ppermute | solution.py:18
  66.1 9.5 %collective-permute-start.18 = (bf16[10,8,256]{2,1,0:T(8,128)(2,1)S(1)}, bf16[10,8,256]{2,1,0:T(8,128)(2,1)S(1)}, u32[]{:S(2)}, u32[]{:S(2)}) collective-permute-start(bf16[10,8,256]{2,1,0:T(8,128)(2,1)S(1)} %get-tuple-element.29), channel_id=1, source_target_pairs={{0,16},{16,32},{32,48},{48,64},{64,80},{80,96},{96,112},{112,128},... | collective-permute-start | bytes 122888 | tf_op jit(solution)/shard_map/ppermute | solution.py:17
  69.5 7.9 %collective-permute-start.4 = (bf16[10,8,1024]{2,1,0:T(8,128)(2,1)S(1)}, bf16[10,8,1024]{2,1,0:T(8,128)(2,1)S(1)}, u32[]{:S(2)}, u32[]{:S(2)}) collective-permute-start(bf16[10,8,1024]{2,1,0:T(8,128)(2,1)S(1)} %get-tuple-element.16), channel_id=1, source_target_pairs={{16,0},{32,16},{48,32},{64,48},{80,64},{96,80},{112,96},{128,112},... | collective-permute-start | bytes 491528 | tf_op jit(solution)/shard_map/ppermute | solution.py:18
  73.6 8.2 %collective-permute-start.3 = (bf16[10,8,1024]{2,1,0:T(8,128)(2,1)S(1)}, bf16[10,8,1024]{2,1,0:T(8,128)(2,1)S(1)}, u32[]{:S(2)}, u32[]{:S(2)}) collective-permute-start(bf16[10,8,1024]{2,1,0:T(8,128)(2,1)S(1)} %get-tuple-element.15), channel_id=1, source_target_pairs={{0,16},{16,32},{32,48},{48,64},{64,80},{80,96},{96,112},{112,128},... | collective-permute-start | bytes 491528 | tf_op jit(solution)/shard_map/ppermute | solution.py:17
  90.5 10.9 %collective-permute-start.10 = (bf16[32,1024]{1,0:T(8,128)(2,1)S(1)}, bf16[32,1024]{1,0:T(8,128)(2,1)S(1)}, u32[]{:S(2)}, u32[]{:S(2)}) collective-permute-start(bf16[32,1024]{1,0:T(8,128)(2,1)S(1)} %bitcast.203), channel_id=1, source_target_pairs={{0,256},{256,0},{16,272},{272,16},{32,288},{288,32},{48,304},{304,... | collective-permute-start | bytes 196616 | tf_op jit(solution)/shard_map/ppermute | solution.py:30
  93.5 7.9 %collective-permute-start.11 = (bf16[1,32,1024]{2,1,0:T(8,128)(2,1)S(1)}, bf16[1,32,1024]{2,1,0:T(8,128)(2,1)S(1)}, u32[]{:S(2)}, u32[]{:S(2)}) collective-permute-start(bf16[1,32,1024]{2,1,0:T(8,128)(2,1)S(1)} %bitcast.204), channel_id=1, source_target_pairs={{0,1},{1,2},{2,3},{3,4},{4,5},{5,6},{6,7},{7,8},{8,9},{9,10},{10,1... | collective-permute-start | bytes 196616 | tf_op jit(solution)/shard_map/ppermute | solution.py:17
  98.0 7.1 %collective-permute-start.12 = (bf16[1,32,1024]{2,1,0:T(8,128)(2,1)S(1)}, bf16[1,32,1024]{2,1,0:T(8,128)(2,1)S(1)}, u32[]{:S(2)}, u32[]{:S(2)}) collective-permute-start(bf16[1,32,1024]{2,1,0:T(8,128)(2,1)S(1)} %bitcast.205), channel_id=1, source_target_pairs={{1,0},{2,1},{3,2},{4,3},{5,4},{6,5},{7,6},{8,7},{9,8},{10,9},{11,1... | collective-permute-start | bytes 196616 | tf_op jit(solution)/shard_map/ppermute | solution.py:18
  105.1 6.4 %collective-permute-start.14 = (bf16[10,8,1024]{2,1,0:T(8,128)(2,1)S(1)}, bf16[10,8,1024]{2,1,0:T(8,128)(2,1)S(1)}, u32[]{:S(2)}, u32[]{:S(2)}) collective-permute-start(bf16[10,8,1024]{2,1,0:T(8,128)(2,1)S(1)} %get-tuple-element.14), channel_id=1, source_target_pairs={{16,0},{32,16},{48,32},{64,48},{80,64},{96,80},{112,96},{128,112},... | collective-permute-start | bytes 491528 | tf_op jit(solution)/shard_map/ppermute | solution.py:18
  107.1 8.2 %collective-permute-start.13 = (bf16[10,8,1024]{2,1,0:T(8,128)(2,1)S(1)}, bf16[10,8,1024]{2,1,0:T(8,128)(2,1)S(1)}, u32[]{:S(2)}, u32[]{:S(2)}) collective-permute-start(bf16[10,8,1024]{2,1,0:T(8,128)(2,1)S(1)} %get-tuple-element.13), channel_id=1, source_target_pairs={{0,16},{16,32},{32,48},{48,64},{64,80},{80,96},{96,112},{112,128},... | collective-permute-start | bytes 491528 | tf_op jit(solution)/shard_map/ppermute | solution.py:17
  (12 other events, 47.5 us)
Sparse Core Ops, SparseCore 0:
  101.5 469.3 all-reduce.4
where the time goes:
time: 582 us; the launch traced here: 581 us
  waiting for transfers between devices  468 us (80%)
  starting transfers between devices  68.7 us (12%)
  local copies, waits for them, and re-layouts  19 us (3%)
  between operations  14.8 us (3%)
  matrix products  9.74 us (2%)
    psum x1, waiting for transfers between devices, local(): grad_one = lax.psum(part_one, ('lon', 'lat'))  447 us
    ppermute x8, starting transfers between devices, extended_2(): after = lax.ppermute(leading, axis, down)  28.6 us
    ppermute x8, starting transfers between devices, extended_2(): before = lax.ppermute(last, axis, up)  28.5 us
    ppermute x8, waiting for transfers between devices, extended_2(): before = lax.ppermute(last, axis, up)  11.8 us
    another operation x12, local copies, waits for them, and re-layouts, band_adjoint(): jnp.stack([extended[2:row_count + 2], extended[1:row_count + 1], extended...  11.7 us
  transfers between devices with their start and end apart: 21, of which 8 were waited for; matrix products, arithmetic and copies ran while one was open for 2% of the time, Pallas kernels for 0%

commit v1 on v0

v1 whole, which is shorter than its diff:
```python
import functools

import jax
import jax.numpy as jnp
from jax import lax
from jax.experimental import pallas as pl
from jax.experimental.pallas import tpu as pltpu
from jax.sharding import PartitionSpec as P

GELU_C = 0.7978845608028654
CUBIC = 0.044715
MESH = pl.DeviceIdType.MESH

ROWS, COLS, CH, KB, REACH = 8, 32, 256, 4, 8
HALO = 2 * REACH
XR, XC = ROWS + 4, COLS + 2 * HALO
MR, MC = ROWS + 2, COLS + 2 * REACH
TAP = 3 * XC
HALF = KB * CH // 2


def dot(a, b):
    return jnp.dot(a, b, preferred_element_type=jnp.float32)


def dot_t(a, b):
    return lax.dot_general(a, b, (((1,), (1,)), ((), ())), preferred_element_type=jnp.float32)


def t_dot(a, b):
    return lax.dot_general(a, b, (((0,), (0,)), ((), ())), preferred_element_type=jnp.float32)


def loop(count, body):
    lax.fori_loop(0, count, lambda i, c: (body(i), c)[1], 0, unroll=True)


def kernel(
    nlat,
    nlon,
    grid_ref,
    tab_ref,
    w1_ref,
    w2_ref,
    cot_ref,
    gin_ref,
    out1_ref,
    out2_ref,
    gext,
    cext,
    fband,
    aband,
    w1,
    w2,
    zbuf,
    z1own,
    z2,
    slope,
    hid,
    gact,
    gown,
    part1,
    part2,
    crecv,
    xsend,
    xrecv,
    zown,
    zrecv,
    zall,
    local_sem,
    halo_send,
    halo_recv,
    core_send,
    core_recv,
    x_send,
    x_recv,
    z_send,
    z_recv,
    zg_send,
    zg_recv,
    xg_send,
    xg_recv,
    f_send,
    f_recv,
):
    nx, nz = nlat // 4, nlon // 2
    npl = nx * 4
    xr = HALF // npl
    zr = 2 * xr // nz
    zh = nz // 2
    lat, lon = lax.axis_index("lat"), lax.axis_index("lon")
    core = lat % 2
    z = lon % nz
    me = (lat // 2) * 2 + lon // nz

    def at(la, lo):
        return {"lat": la, "lon": lo}

    def in_plane(q):
        return at((q // 2) * 2 + core, (q % 2) * nz + z)

    def in_z(q):
        return at(lat, (lon // nz) * nz + q)

    north = (lat == 0).astype(jnp.int32)
    south = (lat == nlat - 1).astype(jnp.int32)
    turn = nlon // 2
    up = (lat - 1 + north, (lon + turn * north) % nlon)
    down = (lat + 1 - south, (lon + turn * south) % nlon)
    west, east = (lon + nlon - 1) % nlon, (lon + 1) % nlon
    sibling = at(lat + 1 - 2 * core, lon)

    def beside(place, step):
        return at(place[0], (place[1] + nlon + step) % nlon)

    up_row = (XR - 2) * (1 - north)
    down_row = (XR - 2) * south
    neighbours = [
        (at(lat, west), slice(0, ROWS), slice(0, HALO), 2, ROWS, COLS + HALO, HALO),
        (at(lat, east), slice(0, ROWS), slice(COLS - HALO, COLS), 2, ROWS, 0, HALO),
        (at(*up), slice(0, 2), slice(0, COLS), up_row, 2, HALO, COLS),
        (at(*down), slice(ROWS - 2, ROWS), slice(0, COLS), down_row, 2, HALO, COLS),
        (beside(up, -1), slice(0, 2), slice(0, HALO), up_row, 2, COLS + HALO, HALO),
        (beside(up, 1), slice(0, 2), slice(COLS - HALO, COLS), up_row, 2, 0, HALO),
        (beside(down, -1), slice(ROWS - 2, ROWS), slice(0, HALO), down_row, 2, COLS + HALO, HALO),
        (beside(down, 1), slice(ROWS - 2, ROWS), slice(COLS - HALO, COLS), down_row, 2, 0, HALO),
    ]

    own = (
        pltpu.make_async_copy(
            grid_ref, gext.at[pl.ds(2, ROWS), pl.ds(HALO, COLS)], local_sem.at[0]
        ),
        pltpu.make_async_copy(cot_ref, cext.at[pl.ds(2, ROWS), pl.ds(HALO, COLS)], local_sem.at[1]),
        pltpu.make_async_copy(w1_ref, w1, local_sem.at[2]),
        pltpu.make_async_copy(w2_ref, w2, local_sem.at[3]),
    )
    for copy in own:
        copy.start()

    barrier = pltpu.get_barrier_semaphore()

    def greet(device):
        pl.semaphore_signal(barrier, inc=1, device_id=device, device_id_type=MESH)

    for device, *_ in neighbours:
        greet(device)
    greet(sibling)
    loop(npl - 1, lambda i: greet(in_plane((me + 1 + i) % npl)))
    loop(nz - 1, lambda i: greet(in_z((z + 1 + i) % nz)))
    pl.semaphore_wait(barrier, len(neighbours) + 1 + npl - 1 + nz - 1)

    for which, (src, ext) in enumerate(((grid_ref, gext), (cot_ref, cext))):
        for device, rows, cols, row, count, col, width in neighbours:
            pltpu.make_async_remote_copy(
                src_ref=src.at[rows, cols],
                dst_ref=ext.at[pl.ds(row, count), pl.ds(col, width)],
                send_sem=halo_send.at[which],
                recv_sem=halo_recv.at[which],
                device_id=device,
                device_id_type=MESH,
            ).start()

    def await_bytes(ref, sem):
        pltpu.make_async_copy(ref, ref, sem).wait()

    def build(which, band):
        def one(v):
            for k in range(KB):
                for h in range(2):
                    taps = tab_ref[which, v, pl.ds(2 * k + h, 1), :]
                    taps = jnp.broadcast_to(taps, (MC, 128))
                    rolled = pltpu.roll(taps, 0, 1, stride=1, stride_axis=0)
                    band[v, k * MC : (k + 1) * MC, h * 128 : (h + 1) * 128] = rolled.astype(
                        jnp.bfloat16
                    )

        loop(MR, one)

    build(0, fband)
    build(1, aband)
    for buf in (hid, gact):
        buf[:, MC:XC, :] = jnp.zeros((MR, XC - MC, CH), jnp.bfloat16)

    def slot(v):
        if v < 2:
            return v + north * (1 - 2 * v)
        if v >= XR - 2:
            return v + south * (2 * (XR - 2) + 1 - 2 * v)
        return v

    def conv_wide(ext, band, keep_own):
        for v in range(MR):
            rows = jnp.concatenate([ext[slot(v + r)] for r in range(3)], axis=0)
            full = dot(band[v, :, :TAP], rows)
            mixed = full.astype(jnp.bfloat16)
            for k in range(KB):
                zbuf[v * MC : (v + 1) * MC, k * CH : (k + 1) * CH] = mixed[
                    k * MC : (k + 1) * MC, :
                ]
            if keep_own and 1 <= v <= ROWS:
                for k in range(KB):
                    z1own[k, (v - 1) * COLS : v * COLS, :] = full[
                        k * MC + REACH : k * MC + REACH + COLS, :
                    ].astype(jnp.bfloat16)

    def conv_own(src, band, store):
        for i in range(ROWS):
            taps = jnp.concatenate(
                [band[i + 1, k * MC : k * MC + COLS, :TAP] for k in range(KB)], axis=0
            )
            rows = src[i : i + 3].reshape(TAP, CH)
            mixed = dot(taps, rows).astype(jnp.bfloat16)
            for k in range(KB):
                store(i, k, mixed[k * COLS : (k + 1) * COLS, :])

    own[0].wait()
    await_bytes(gext.at[pl.ds(0, ROWS)], halo_recv.at[0])
    conv_wide(gext, fband, True)
    own[2].wait()
    act = dot(zbuf[...], w1[...].reshape(KB * CH, CH))
    tanh_val = jnp.tanh(GELU_C * (act + CUBIC * act * act * act))
    slope[...] = 0.5 * (1.0 + tanh_val) + 0.5 * act * (1.0 - tanh_val * tanh_val) * GELU_C * (
        1.0 + 3.0 * CUBIC * act * act
    )
    hidden = (0.5 * act * (1.0 + tanh_val)).astype(jnp.bfloat16)
    for v in range(MR):
        hid[v, :MC, :] = hidden[v * MC : (v + 1) * MC, :]

    def weight_grad(cells, grad, part, g):
        for step in range(KB):
            k = (2 * (1 - core) + step) % KB
            part[k] = t_dot(cells[k], grad)
            if step < 2:
                pltpu.make_async_remote_copy(
                    src_ref=part.at[k],
                    dst_ref=crecv.at[g, step],
                    send_sem=core_send.at[g],
                    recv_sem=core_recv.at[g],
                    device_id=sibling,
                    device_id_type=MESH,
                ).start()

    def store_z2(i, k, value):
        z2[k, i * COLS : (i + 1) * COLS, :] = value

    conv_own(hid, fband, store_z2)
    own[1].wait()
    weight_grad(z2, cext[2 : 2 + ROWS, HALO : HALO + COLS, :].reshape(ROWS * COLS, CH), part2, 1)

    def mix_back(cells, weight):
        total = dot_t(cells[:, :CH], weight[0])
        for k in range(1, KB):
            total = total + dot_t(cells[:, k * CH : (k + 1) * CH], weight[k])
        return total

    await_bytes(cext.at[pl.ds(0, ROWS)], halo_recv.at[1])
    conv_wide(cext, aband, False)
    own[3].wait()
    grad_act = mix_back(zbuf, w2) * slope[...]
    for v in range(MR):
        gact[v, :MC, :] = grad_act[v * MC : (v + 1) * MC, :].astype(jnp.bfloat16)
        if 1 <= v <= ROWS:
            gown[(v - 1) * COLS : v * COLS, :] = grad_act[
                v * MC + REACH : v * MC + REACH + COLS, :
            ].astype(jnp.bfloat16)
    weight_grad(z1own, gown[...], part1, 0)

    parts = (part1, part2)
    outs = (out1_ref, out2_ref)
    own_half = 2 * core

    def plane_chunk(g, q):
        k, row = q * xr // CH, (q * xr) % CH
        row = pl.multiple_of(row, xr)
        return parts[g][own_half + k, pl.ds(row, xr), :] + crecv[g, k, pl.ds(row, xr), :]

    def plane_scatter(g):
        await_bytes(crecv.at[g], core_recv.at[g])

        def one(i):
            q = (me + 1 + i) % npl
            xsend[g, i] = plane_chunk(g, q).astype(jnp.bfloat16)
            pltpu.make_async_remote_copy(
                src_ref=xsend.at[g, i],
                dst_ref=xrecv.at[g, i],
                send_sem=x_send.at[g],
                recv_sem=x_recv.at[g],
                device_id=in_plane(q),
                device_id_type=MESH,
            ).start()

        loop(npl - 1, one)

    def z_scatter(g):
        total = plane_chunk(g, me)
        await_bytes(xrecv.at[g], x_recv.at[g])
        for i in range(npl - 1):
            total = total + xrecv[g, i].astype(jnp.float32)
        for q in range(nz):
            zown[g, q] = total[
                (q % zh) * zr : (q % zh + 1) * zr, (q // zh) * 128 : (q // zh + 1) * 128
            ]

        def one(i):
            q = (z + 1 + i) % nz
            pltpu.make_async_remote_copy(
                src_ref=zown.at[g, q],
                dst_ref=zrecv.at[g, i],
                send_sem=z_send.at[g],
                recv_sem=z_recv.at[g],
                device_id=in_z(q),
                device_id_type=MESH,
            ).start()

        loop(nz - 1, one)

    def z_gather(g):
        total = zown[g, z]
        await_bytes(zrecv.at[g], z_recv.at[g])
        for i in range(nz - 1):
            total = total + zrecv[g, i]
        zall[g, z] = total

        def one(i):
            pltpu.make_async_remote_copy(
                src_ref=zall.at[g, z],
                dst_ref=zall.at[g, z],
                send_sem=zg_send.at[g],
                recv_sem=zg_recv.at[g],
                device_id=in_z((z + 1 + i) % nz),
                device_id_type=MESH,
            ).start()

        loop(nz - 1, one)

    def plane_gather(g):
        await_bytes(zall.at[g, pl.ds(0, nz - 1)], zg_recv.at[g])
        left = jnp.concatenate([zall[g, q] for q in range(zh)], axis=0)
        right = jnp.concatenate([zall[g, zh + q] for q in range(zh)], axis=0)
        rows = pl.ds(pl.multiple_of(core * HALF + me * xr, xr), xr)
        out = outs[g]
        out[rows, :] = jnp.concatenate([left, right], axis=1).astype(jnp.bfloat16)

        def one(i):
            pltpu.make_async_remote_copy(
                src_ref=out.at[rows],
                dst_ref=out.at[rows],
                send_sem=xg_send.at[g],
                recv_sem=xg_recv.at[g],
                device_id=in_plane((me + 1 + i) % npl),
                device_id_type=MESH,
            ).start()

        loop(npl - 1, one)

    def core_gather(g):
        out = outs[g]
        await_bytes(out.at[pl.ds(0, (npl - 1) * xr)], xg_recv.at[g])
        rows = pl.ds(pl.multiple_of(core * HALF, HALF), HALF)
        pltpu.make_async_remote_copy(
            src_ref=out.at[rows],
            dst_ref=out.at[rows],
            send_sem=f_send.at[g],
            recv_sem=f_recv.at[g],
            device_id=sibling,
            device_id_type=MESH,
        ).start()

    plane_scatter(1)
    plane_scatter(0)

    def store_back(i, k, value):
        zbuf[i * COLS : (i + 1) * COLS, k * CH : (k + 1) * CH] = value

    conv_own(gact, aband, store_back)
    gin_ref[...] = mix_back(zbuf.at[pl.ds(0, ROWS * COLS)], w1)

    z_scatter(1)
    z_scatter(0)
    z_gather(1)
    z_gather(0)
    plane_gather(1)
    plane_gather(0)
    core_gather(1)
    core_gather(0)
    for which, ext in enumerate((gext, cext)):
        await_bytes(ext.at[pl.ds(0, ROWS)], halo_send.at[which])
    for g in range(2):
        await_bytes(crecv.at[g], core_send.at[g])
        await_bytes(xrecv.at[g], x_send.at[g])
        await_bytes(zrecv.at[g], z_send.at[g])
        await_bytes(zall.at[g, pl.ds(0, nz - 1)], zg_send.at[g])
        await_bytes(outs[g].at[pl.ds(0, (npl - 1) * xr)], xg_send.at[g])
    for g in range(2):
        await_bytes(outs[g].at[pl.ds(0, HALF)], f_recv.at[g])
        await_bytes(outs[g].at[pl.ds(0, HALF)], f_send.at[g])


def tap_table(basis, widths):
    span = basis.shape[2]
    keep = jnp.abs(jnp.arange(span) - REACH)[None, :] <= widths[:, None]
    masked = jnp.where(keep[:, None, :, None], basis.astype(jnp.float32), 0.0)
    masked = jnp.concatenate([masked[1::-1, ::-1], masked, masked[:-3:-1, ::-1]], axis=0)
    rows = lax.dynamic_slice_in_dim(masked, lax.axis_index("lat") * ROWS, XR, 0)
    forward = rows[1 : 1 + MR]
    back = jnp.stack([rows[s : s + MR, 2 - s, ::-1] for s in range(3)], axis=1)
    both = jnp.stack([forward, back]).transpose(0, 1, 4, 2, 3)
    both = jnp.pad(both, ((0, 0), (0, 0), (0, 0), (0, 1), (0, XC - span)))
    return both.reshape(2, MR, 2 * KB, 128)


def local(grid_in, basis, widths, weight_one, weight_two, cotangent):
    nlat, nlon = lax.axis_size("lat"), lax.axis_size("lon")
    npl, nz = nlat, nlon // 2
    xr = HALF // npl
    zr = 2 * xr // nz
    bf16, f32 = jnp.bfloat16, jnp.float32
    vmem, dma = pltpu.VMEM, pltpu.SemaphoreType.DMA
    hbm = pl.BlockSpec(memory_space=pl.ANY)
    on_chip = pl.BlockSpec(memory_space=pltpu.VMEM)
    grad_in, one, two = pl.pallas_call(
        functools.partial(kernel, nlat, nlon),
        out_shape=(
            jax.ShapeDtypeStruct((ROWS * COLS, CH), f32),
            jax.ShapeDtypeStruct((KB * CH, CH), bf16),
            jax.ShapeDtypeStruct((KB * CH, CH), bf16),
        ),
        in_specs=[hbm, on_chip, hbm, hbm, hbm],
        out_specs=(on_chip, on_chip, on_chip),
        scratch_shapes=[
            vmem((XR, XC, CH), bf16),
            vmem((XR, XC, CH), bf16),
            vmem((MR, KB * MC, 256), bf16),
            vmem((MR, KB * MC, 256), bf16),
            vmem((KB, CH, CH), bf16),
            vmem((KB, CH, CH), bf16),
            vmem((MR * MC, KB * CH), bf16),
            vmem((KB, ROWS * COLS, CH), bf16),
            vmem((KB, ROWS * COLS, CH), bf16),
            vmem((MR * MC, CH), f32),
            vmem((MR, XC, CH), bf16),
            vmem((MR, XC, CH), bf16),
            vmem((ROWS * COLS, CH), bf16),
            vmem((KB, CH, CH), f32),
            vmem((KB, CH, CH), f32),
            vmem((2, 2, CH, CH), f32),
            vmem((2, npl - 1, xr, CH), bf16),
            vmem((2, npl - 1, xr, CH), bf16),
            vmem((2, nz, zr, 128), f32),
            vmem((2, nz - 1, zr, 128), f32),
            vmem((2, nz, zr, 128), f32),
            dma((4,)),
        ]
        + [dma((2,))] * 14,
        compiler_params=pltpu.CompilerParams(
            collective_id=0, has_side_effects=True, vmem_limit_bytes=48 * 1024 * 1024
        ),
    )(grid_in, tap_table(basis, widths), weight_one, weight_two, cotangent)
    shape = weight_one.shape
    return (
        grad_in.reshape(grid_in.shape),
        one.astype(f32).reshape(shape),
        two.astype(f32).reshape(shape),
    )


def solution(mesh):
    placed = (P("lat", "lon", None), P(), P(), P(), P(), P("lat", "lon", None))
    return jax.shard_map(
        local,
        mesh=mesh,
        in_specs=placed,
        out_specs=(P("lat", "lon", None), P(), P()),
        check_vma=False,
    )
```

time: 582 us -> 69.2 us (0.12)
  waiting for transfers between devices: 468 us -> 0 us
  starting transfers between devices: 68.7 us -> 0 us
  Pallas kernels: 0 us -> 61.6 us
  local copies, waits for them, and re-layouts: 19 us -> 3.22 us
  between operations: 14.8 us -> 0.76 us
  matrix products: 9.74 us -> 0 us
    psum x1 -> x0, waiting for transfers between devices: 447 us -> none  [local(): grad_one = lax.psum(part_one, ('lon', 'lat'))]
    ppermute x20 -> x0, starting transfers between devices: 68.6 us -> none  [the longest x8 28.6 us: extended_2(): after = lax.ppermute(leading, axis, down)]
    pallas_call x0 -> x1, Pallas kernels: none -> 61.6 us  [local(): pl.pallas_call(functools.partial(kernel, nlat, nlon), out_shape=(jax.Shap...]
    ppermute x20 -> x0, waiting for transfers between devices: 21.5 us -> none  [the longest x8 11.8 us: extended_2(): before = lax.ppermute(last, axis, up)]
    another operation x16 -> x0, local copies, waits for them, and re-layouts: 11.8 us -> none  [the longest x12 11.7 us: band_adjoint(): jnp.stack([extended[2:row_count + 2], extended[1:row_count + 1], extended...]
    dot_general x10 -> x0, matrix products: 9.74 us -> none  [the longest x2 1.9 us: band_adjoint(): jnp.einsum('prkjm,prmkc->pjc', adjoint_band, stacked, preferred_element_t...]
  transfers between devices with their start and end apart: 21 -> 0, of which waited for: 8 -> 0; matrix products, arithmetic and copies ran while one was open for 2% -> 0% of each run, Pallas kernels for 0% -> 0%
where the time goes in v1:
time: 69.2 us; the launch traced here: 69 us
  Pallas kernels  61.6 us (89%)
  other arithmetic  3.45 us (5%)
  local copies, waits for them, and re-layouts  3.22 us (5%)
  between operations  0.76 us (1%)
    pallas_call x1, Pallas kernels, local(): pl.pallas_call(functools.partial(kernel, nlat, nlon), out_shape=(jax.Shap...  61.6 us
    unnamed x12, local copies, waits for them, and re-layouts  2.5 us

profile of v1, /device:TPU:1, one launch (start us, length us, event | category | flops | bytes accessed | tf_op | source)
XLA Modules:
  0.0 69.0 jit_solution(11475704615669158808)
XLA Ops:
  0.6 0.0 copy-start.4
  0.7 0.6 copy-done.4
  1.3 0.1 broadcast_compare_fusion
  1.4 0.8 %convert_select_fusion = f32[128,3,17,4]{0,3,2,1:T(4,128)S(1)} fusion(bf16[128,3,17,4]{0,3,2,1:T(4,128)(2,1)} %param.7, pred[128,17]{0,1:T(8,128)(4,1)S(1)} %broadcast_compare_fusion), kind=kLoop, calls=%fused_computation.8 | loop fusion | flops 52224 | bytes 158848 | tf_op jit(solution)/shard_map/jit(_where)/select_n | solution.py:402
  2.2 0.1 fusion.3
  2.3 0.2 rev.16
  2.5 0.2 rev.15
  2.7 0.2 fusion.1
  2.9 0.1 fusion.2
  3.1 0.1 slice_bitcast_fusion
  3.2 0.0 copy-start.1
  3.2 0.1 maximum_bitcast_fusion
  3.3 0.0 copy-start
  3.3 0.3 copy.10
  3.6 0.0 copy-start.2
  3.6 0.1 reshape.55.tab_ref
  3.7 0.5 copy-done.1
  4.2 0.2 copy-done
  4.4 0.2 copy-done.3
  4.6 0.0 copy-done.2
  4.6 61.6 %shard_map.85 = (f32[256,256]{1,0:T(8,128)S(1)}, bf16[1024,256]{1,0:T(8,128)(2,1)S(1)}, bf16[1024,256]{1,0:T(8,128)(2,1)S(1)}) custom-call(bf16[8,32,256]{2,1,0:T(8,128)(2,1)S(1)} %copy-done.2, f32[2,10,8,128]{3,2,1,0:T(8,128)S(1)} %reshape.55.tab_ref, bf16[4,256,256]{2,1,0:T(8,128)(2,1)S(1)} %copy-done, bf16[4,256,256]{2,1,0:T(8,128)(2,1)S(1)} %copy-done.1, ...), custom_call_target="tpu_custom_call" | custom-call | tf_op jit(solution)/shard_map/pallas_call | solution.py:421
  66.2 1.1 %convert.2 = f32[4,256,256]{2,1,0:T(8,128)} convert(bf16[4,256,256]{2,1,0:T(8,128)(2,1)S(1)} %bitcast.12) | non-fusion elementwise | flops 262144 | bytes 1572864 | tf_op jit(solution)/shard_map/reshape | solution.py:462
  67.3 1.1 %convert.3 = f32[4,256,256]{2,1,0:T(8,128)} convert(bf16[4,256,256]{2,1,0:T(8,128)(2,1)S(1)} %bitcast.11) | non-fusion elementwise | flops 262144 | bytes 1572864 | tf_op jit(solution)/shard_map/reshape | solution.py:463
  68.3 0.7 %copy.12 = f32[8,32,256]{2,1,0:T(8,128)} copy(f32[8,32,256]{2,1,0:T(8,128)S(1)} %bitcast.13) | data formatting | bytes 524288
  (6 shorter events, 0.1 us)
Async XLA Ops:
  0.6 0.7 copy-start.4
  3.2 1.0 %copy-start.1 = (bf16[4,256,256]{2,1,0:T(8,128)(2,1)S(1)}, bf16[4,256,256]{2,1,0:T(8,128)(2,1)}, u32[]{:S(2)}) copy-start(bf16[4,256,256]{2,1,0:T(8,128)(2,1)} %w2_ref.1) | copy-start | bytes 1572868
  3.3 1.1 %copy-start = (bf16[4,256,256]{2,1,0:T(8,128)(2,1)S(1)}, bf16[4,256,256]{2,1,0:T(8,128)(2,1)}, u32[]{:S(2)}) copy-start(bf16[4,256,256]{2,1,0:T(8,128)(2,1)} %w1_ref.1) | copy-start | bytes 1572868
  3.6 1.0 %copy-start.3 = (bf16[8,32,256]{2,1,0:T(8,128)(2,1)S(1)}, bf16[8,32,256]{2,1,0:T(8,128)(2,1)}, u32[]{:S(2)}) copy-start(bf16[8,32,256]{2,1,0:T(8,128)(2,1)} %cot_ref.1) | copy-start | bytes 393220
  3.6 1.0 %copy-start.2 = (bf16[8,32,256]{2,1,0:T(8,128)(2,1)S(1)}, bf16[8,32,256]{2,1,0:T(8,128)(2,1)}, u32[]{:S(2)}) copy-start(bf16[8,32,256]{2,1,0:T(8,128)(2,1)} %grid_ref.1) | copy-start | bytes 393220

commit v2 on v1

--- a/solution.py
+++ b/solution.py
@@ -16,6 +16,9 @@
 XR, XC = ROWS + 4, COLS + 2 * HALO
 MR, MC = ROWS + 2, COLS + 2 * REACH
 TAP = 3 * XC
+SPAN = 2 * REACH + 1
+TAPS = 64
+SLOT = 16
 HALF = KB * CH // 2
 
 
@@ -33,13 +36,74 @@
 
 def loop(count, body):
     lax.fori_loop(0, count, lambda i, c: (body(i), c)[1], 0, unroll=True)
+
+
+def ring_steps(count):
+    return sorted(range(1, count), key=lambda d: -min(d, count - d))
+
+
+def plane_steps(nx, ny):
+    steps = [(dx, dy) for dx in range(nx) for dy in range(ny) if dx or dy]
+    return sorted(steps, key=lambda s: -min(s[0], nx - s[0]) - min(s[1], ny - s[1]))
+
+
+def iota(rows, cols, axis):
+    return lax.broadcasted_iota(jnp.int32, (rows, cols), axis)
+
+
+def one_hot(where):
+    return where.astype(jnp.float32).astype(jnp.bfloat16)
+
+
+def spread_taps(basis_ref, widths_ref, taps, tab, lat, nlat_all):
+    zeros = jnp.zeros((KB * TAPS, nlat_all), jnp.float32)
+    taps[0], taps[1] = zeros, zeros
+    widths = widths_ref[...]
+    for r in range(3):
+        for s in range(SPAN):
+            block = basis_ref[r * SPAN + s].astype(jnp.float32)
+            block = jnp.where(widths >= abs(s - REACH), block, 0.0)
+            taps[0, pl.ds(r * SPAN + s, KB, stride=TAPS), :] = block
+            taps[1, pl.ds((2 - r) * SPAN + s, KB, stride=TAPS), :] = block
+    picks = []
+    for j in range(3):
+        row = lat * ROWS - 2 + j + iota(SLOT, nlat_all, 0)
+        past = (row < 0) | (row >= nlat_all)
+        true_row = jnp.where(row < 0, -1 - row, jnp.where(past, 2 * nlat_all - 1 - row, row))
+        hit = true_row == iota(SLOT, nlat_all, 1)
+        picks.append((one_hot(hit & jnp.logical_not(past)), one_hot(hit & past)))
+    plain = jnp.concatenate([p for p, _ in picks], axis=0)
+    mirror = jnp.concatenate([m for _, m in picks], axis=0)
+    found = []
+    for k in range(KB):
+        rows = slice(k * TAPS, (k + 1) * TAPS)
+        found.append(
+            dot_t(plain, taps[0, rows, :].astype(jnp.bfloat16))
+            + dot_t(mirror, taps[1, rows, :].astype(jnp.bfloat16))
+        )
+
+    def of(j):
+        parts = [f[j * SLOT : (j + 1) * SLOT, :] for f in found]
+        return jnp.concatenate(parts, axis=0).astype(jnp.bfloat16)
+
+    source, lane = iota(TAPS, 4 * XC, 0), iota(TAPS, 4 * XC, 1)
+    r, s = lane // XC, lane % XC
+    used = (s < SPAN) & (r < 3)
+    tab[0] = dot(of(1), one_hot(used & (source == r * SPAN + s)))
+    total = None
+    for j in range(3):
+        place = one_hot(used & (r == j) & (source == (2 - j) * SPAN + SPAN - 1 - s))
+        part = dot(of(j), place)
+        total = part if total is None else total + part
+    tab[1] = total
 
 
 def kernel(
     nlat,
     nlon,
     grid_ref,
-    tab_ref,
+    basis_ref,
+    widths_ref,
     w1_ref,
     w2_ref,
     cot_ref,
@@ -48,6 +112,10 @@
     out2_ref,
     gext,
     cext,
+    basis,
+    widths,
+    taps,
+    tab,
     fband,
     aband,
     w1,
@@ -82,6 +150,7 @@
     xg_recv,
     f_send,
     f_recv,
+    z_known,
 ):
     nx, nz = nlat // 4, nlon // 2
     npl = nx * 4
@@ -96,18 +165,28 @@
     def at(la, lo):
         return {"lat": la, "lon": lo}
 
+    plane, line = plane_steps(nx, 4), ring_steps(nz)
+
+    def plane_place(step):
+        return ((me // 4 + step[0]) % nx) * 4 + (me + step[1]) % 4
+
     def in_plane(q):
         return at((q // 2) * 2 + core, (q % 2) * nz + z)
 
     def in_z(q):
         return at(lat, (lon // nz) * nz + q)
+
+    reach = 1
+    z_rounds = []
+    while 2 * reach < nz:
+        z_rounds.append(reach)
+        reach *= 2
 
     north = (lat == 0).astype(jnp.int32)
     south = (lat == nlat - 1).astype(jnp.int32)
     turn = nlon // 2
     up = (lat - 1 + north, (lon + turn * north) % nlon)
     down = (lat + 1 - south, (lon + turn * south) % nlon)
-    west, east = (lon + nlon - 1) % nlon, (lon + 1) % nlon
     sibling = at(lat + 1 - 2 * core, lon)
 
     def beside(place, step):
@@ -115,15 +194,18 @@
 
     up_row = (XR - 2) * (1 - north)
     down_row = (XR - 2) * south
+    first, last = slice(0, 2), slice(ROWS - 2, ROWS)
+    left, right, every = slice(0, HALO), slice(COLS - HALO, COLS), slice(0, COLS)
+    side = (lat, lon)
     neighbours = [
-        (at(lat, west), slice(0, ROWS), slice(0, HALO), 2, ROWS, COLS + HALO, HALO),
-        (at(lat, east), slice(0, ROWS), slice(COLS - HALO, COLS), 2, ROWS, 0, HALO),
-        (at(*up), slice(0, 2), slice(0, COLS), up_row, 2, HALO, COLS),
-        (at(*down), slice(ROWS - 2, ROWS), slice(0, COLS), down_row, 2, HALO, COLS),
-        (beside(up, -1), slice(0, 2), slice(0, HALO), up_row, 2, COLS + HALO, HALO),
-        (beside(up, 1), slice(0, 2), slice(COLS - HALO, COLS), up_row, 2, 0, HALO),
-        (beside(down, -1), slice(ROWS - 2, ROWS), slice(0, HALO), down_row, 2, COLS + HALO, HALO),
-        (beside(down, 1), slice(ROWS - 2, ROWS), slice(COLS - HALO, COLS), down_row, 2, 0, HALO),
+        (beside(up, -1), first, left, up_row, 2, COLS + HALO, HALO),
+        (beside(up, 1), first, right, up_row, 2, 0, HALO),
+        (beside(down, -1), last, left, down_row, 2, COLS + HALO, HALO),
+        (beside(down, 1), last, right, down_row, 2, 0, HALO),
+        (at(*up), first, every, up_row, 2, HALO, COLS),
+        (at(*down), last, every, down_row, 2, HALO, COLS),
+        (beside(side, -1), slice(0, ROWS), left, 2, ROWS, COLS + HALO, HALO),
+        (beside(side, 1), slice(0, ROWS), right, 2, ROWS, 0, HALO),
     ]
 
     own = (
@@ -133,21 +215,35 @@
         pltpu.make_async_copy(cot_ref, cext.at[pl.ds(2, ROWS), pl.ds(HALO, COLS)], local_sem.at[1]),
         pltpu.make_async_copy(w1_ref, w1, local_sem.at[2]),
         pltpu.make_async_copy(w2_ref, w2, local_sem.at[3]),
+        pltpu.make_async_copy(basis_ref, basis, local_sem.at[4]),
+        pltpu.make_async_copy(widths_ref, widths, local_sem.at[5]),
     )
+    barrier = pltpu.get_barrier_semaphore()
+
+    def signal(device, sem):
+        pl.semaphore_signal(sem, inc=1, device_id=device, device_id_type=MESH)
+
+    near = [device for device, *_ in neighbours]
+    near += [sibling] + [in_plane(plane_place(step)) for step in plane]
+    near += [in_z((z + d) % nz) for d in (line if nz < 4 else (1, nz - 1))]
+    for device in near:
+        signal(device, barrier)
     for copy in own:
         copy.start()
-
-    barrier = pltpu.get_barrier_semaphore()
-
-    def greet(device):
-        pl.semaphore_signal(barrier, inc=1, device_id=device, device_id_type=MESH)
-
-    for device, *_ in neighbours:
-        greet(device)
-    greet(sibling)
-    loop(npl - 1, lambda i: greet(in_plane((me + 1 + i) % npl)))
-    loop(nz - 1, lambda i: greet(in_z((z + 1 + i) % nz)))
-    pl.semaphore_wait(barrier, len(neighbours) + 1 + npl - 1 + nz - 1)
+    pl.semaphore_wait(barrier, len(near))
+
+    def z_signal(n):
+        for d in (z_rounds[n], nz - z_rounds[n]):
+            signal(in_z((z + d) % nz), z_known.at[n])
+
+    def z_await(n):
+        if n < len(z_rounds):
+            pl.semaphore_wait(z_known.at[n], 2)
+            if n + 1 < len(z_rounds):
+                z_signal(n + 1)
+
+    if z_rounds:
+        z_signal(0)
 
     for which, (src, ext) in enumerate(((grid_ref, gext), (cot_ref, cext))):
         for device, rows, cols, row, count, col, width in neighbours:
@@ -163,13 +259,18 @@
     def await_bytes(ref, sem):
         pltpu.make_async_copy(ref, ref, sem).wait()
 
+    own[4].wait()
+    own[5].wait()
+    spread_taps(basis, widths, taps, tab, lat, nlat * ROWS)
+
     def build(which, band):
         def one(v):
             for k in range(KB):
                 for h in range(2):
-                    taps = tab_ref[which, v, pl.ds(2 * k + h, 1), :]
-                    taps = jnp.broadcast_to(taps, (MC, 128))
-                    rolled = pltpu.roll(taps, 0, 1, stride=1, stride_axis=0)
+                    row = tab[which, pl.ds(k * SLOT + v, 1), h * 128 : (h + 1) * 128]
+                    rolled = pltpu.roll(
+                        jnp.broadcast_to(row, (MC, 128)), 0, 1, stride=1, stride_axis=0
+                    )
                     band[v, k * MC : (k + 1) * MC, h * 128 : (h + 1) * 128] = rolled.astype(
                         jnp.bfloat16
                     )
@@ -215,6 +316,7 @@
 
     own[0].wait()
     await_bytes(gext.at[pl.ds(0, ROWS)], halo_recv.at[0])
+    z_await(0)
     conv_wide(gext, fband, True)
     own[2].wait()
     act = dot(zbuf[...], w1[...].reshape(KB * CH, CH))
@@ -254,6 +356,7 @@
         return total
 
     await_bytes(cext.at[pl.ds(0, ROWS)], halo_recv.at[1])
+    z_await(1)
     conv_wide(cext, aband, False)
     own[3].wait()
     grad_act = mix_back(zbuf, w2) * slope[...]
@@ -277,8 +380,8 @@
     def plane_scatter(g):
         await_bytes(crecv.at[g], core_recv.at[g])
 
-        def one(i):
-            q = (me + 1 + i) % npl
+        for i, step in enumerate(plane):
+            q = plane_place(step)
             xsend[g, i] = plane_chunk(g, q).astype(jnp.bfloat16)
             pltpu.make_async_remote_copy(
                 src_ref=xsend.at[g, i],
@@ -289,8 +392,6 @@
                 device_id_type=MESH,
             ).start()
 
-        loop(npl - 1, one)
-
     def z_scatter(g):
         total = plane_chunk(g, me)
         await_bytes(xrecv.at[g], x_recv.at[g])
@@ -301,8 +402,8 @@
                 (q % zh) * zr : (q % zh + 1) * zr, (q // zh) * 128 : (q // zh + 1) * 128
             ]
 
-        def one(i):
-            q = (z + 1 + i) % nz
+        for i, d in enumerate(line):
+            q = (z + d) % nz
             pltpu.make_async_remote_copy(
                 src_ref=zown.at[g, q],
                 dst_ref=zrecv.at[g, i],
@@ -312,8 +413,6 @@
                 device_id_type=MESH,
             ).start()
 
-        loop(nz - 1, one)
-
     def z_gather(g):
         total = zown[g, z]
         await_bytes(zrecv.at[g], z_recv.at[g])
@@ -321,17 +420,15 @@
             total = total + zrecv[g, i]
         zall[g, z] = total
 
-        def one(i):
+        for d in line:
             pltpu.make_async_remote_copy(
                 src_ref=zall.at[g, z],
                 dst_ref=zall.at[g, z],
                 send_sem=zg_send.at[g],
                 recv_sem=zg_recv.at[g],
-                device_id=in_z((z + 1 + i) % nz),
+                device_id=in_z((z + d) % nz),
                 device_id_type=MESH,
             ).start()
-
-        loop(nz - 1, one)
 
     def plane_gather(g):
         await_bytes(zall.at[g, pl.ds(0, nz - 1)], zg_recv.at[g])
@@ -341,17 +438,15 @@
         out = outs[g]
         out[rows, :] = jnp.concatenate([left, right], axis=1).astype(jnp.bfloat16)
 
-        def one(i):
+        for step in plane:
             pltpu.make_async_remote_copy(
                 src_ref=out.at[rows],
                 dst_ref=out.at[rows],
                 send_sem=xg_send.at[g],
                 recv_sem=xg_recv.at[g],
-                device_id=in_plane((me + 1 + i) % npl),
+                device_id=in_plane(plane_place(step)),
                 device_id_type=MESH,
             ).start()
-
-        loop(npl - 1, one)
 
     def core_gather(g):
         out = outs[g]
@@ -375,6 +470,7 @@
     conv_own(gact, aband, store_back)
     gin_ref[...] = mix_back(zbuf.at[pl.ds(0, ROWS * COLS)], w1)
 
+    z_await(2)
     z_scatter(1)
     z_scatter(0)
     z_gather(1)
@@ -396,17 +492,16 @@
         await_bytes(outs[g].at[pl.ds(0, HALF)], f_send.at[g])
 
 
-def tap_table(basis, widths):
-    span = basis.shape[2]
-    keep = jnp.abs(jnp.arange(span) - REACH)[None, :] <= widths[:, None]
-    masked = jnp.where(keep[:, None, :, None], basis.astype(jnp.float32), 0.0)
-    masked = jnp.concatenate([masked[1::-1, ::-1], masked, masked[:-3:-1, ::-1]], axis=0)
-    rows = lax.dynamic_slice_in_dim(masked, lax.axis_index("lat") * ROWS, XR, 0)
-    forward = rows[1 : 1 + MR]
-    back = jnp.stack([rows[s : s + MR, 2 - s, ::-1] for s in range(3)], axis=1)
-    both = jnp.stack([forward, back]).transpose(0, 1, 4, 2, 3)
-    both = jnp.pad(both, ((0, 0), (0, 0), (0, 0), (0, 1), (0, XC - span)))
-    return both.reshape(2, MR, 2 * KB, 128)
+def widen(g_ref, a_ref, b_ref, g_out, a_out, b_out, a_buf, b_buf, g_sem, ab_sem):
+    copies = [pltpu.make_async_copy(g_ref, g_out, g_sem)]
+    copies[0].start()
+    for n, (ref, buf, out) in enumerate(((a_ref, a_buf, a_out), (b_ref, b_buf, b_out))):
+        for k in range(KB):
+            buf[k] = ref[k * CH : (k + 1) * CH, :].astype(jnp.float32)
+            copies.append(pltpu.make_async_copy(buf.at[k], out.at[k], ab_sem.at[n, k]))
+            copies[-1].start()
+    for copy in copies:
+        copy.wait()
 
 
 def local(grid_in, basis, widths, weight_one, weight_two, cotangent):
@@ -416,8 +511,18 @@
     zr = 2 * xr // nz
     bf16, f32 = jnp.bfloat16, jnp.float32
     vmem, dma = pltpu.VMEM, pltpu.SemaphoreType.DMA
-    hbm = pl.BlockSpec(memory_space=pl.ANY)
+    hbm = pl.BlockSpec(memory_space=pltpu.HBM)
     on_chip = pl.BlockSpec(memory_space=pltpu.VMEM)
+    nlat_all = basis.shape[0]
+    basis = basis.transpose(1, 2, 3, 0).reshape(3 * SPAN, KB, nlat_all)
+    grid_in, weight_one, weight_two, cotangent = (
+        pltpu.with_memory_space_constraint(x, pltpu.HBM)
+        for x in (grid_in, weight_one, weight_two, cotangent)
+    )
+    basis, widths = (
+        pltpu.with_memory_space_constraint(x, pltpu.HBM)
+        for x in (basis, widths.reshape(1, nlat_all))
+    )
     grad_in, one, two = pl.pallas_call(
         functools.partial(kernel, nlat, nlon),
         out_shape=(
@@ -425,11 +530,15 @@
             jax.ShapeDtypeStruct((KB * CH, CH), bf16),
             jax.ShapeDtypeStruct((KB * CH, CH), bf16),
         ),
-        in_specs=[hbm, on_chip, hbm, hbm, hbm],
+        in_specs=[hbm] * 6,
         out_specs=(on_chip, on_chip, on_chip),
         scratch_shapes=[
             vmem((XR, XC, CH), bf16),
             vmem((XR, XC, CH), bf16),
+            vmem((3 * SPAN, KB, nlat_all), bf16),
+            vmem((1, nlat_all), jnp.int32),
+            vmem((2, KB * TAPS, nlat_all), f32),
+            vmem((2, KB * SLOT, 4 * XC), f32),
             vmem((MR, KB * MC, 256), bf16),
             vmem((MR, KB * MC, 256), bf16),
             vmem((KB, CH, CH), bf16),
@@ -449,19 +558,24 @@
             vmem((2, nz, zr, 128), f32),
             vmem((2, nz - 1, zr, 128), f32),
             vmem((2, nz, zr, 128), f32),
-            dma((4,)),
+            dma((6,)),
         ]
-        + [dma((2,))] * 14,
+        + [dma((2,))] * 14
+        + [pltpu.SemaphoreType.REGULAR((3,))],
         compiler_params=pltpu.CompilerParams(
             collective_id=0, has_side_effects=True, vmem_limit_bytes=48 * 1024 * 1024
         ),
-    )(grid_in, tap_table(basis, widths), weight_one, weight_two, cotangent)
-    shape = weight_one.shape
-    return (
-        grad_in.reshape(grid_in.shape),
-        one.astype(f32).reshape(shape),
-        two.astype(f32).reshape(shape),
-    )
+    )(grid_in, basis, widths, weight_one, weight_two, cotangent)
+    wide = jax.ShapeDtypeStruct(weight_one.shape, f32)
+    grad_in, one, two = pl.pallas_call(
+        widen,
+        out_shape=(jax.ShapeDtypeStruct((ROWS * COLS, CH), f32), wide, wide),
+        in_specs=[on_chip] * 3,
+        out_specs=(hbm, hbm, hbm),
+        scratch_shapes=[vmem(wide.shape, f32), vmem(wide.shape, f32), dma, dma((2, KB))],
+        compiler_params=pltpu.CompilerParams(vmem_limit_bytes=16 * 1024 * 1024),
+    )(grad_in, one, two)
+    return grad_in.reshape(grid_in.shape), one, two
 
 
 def solution(mesh):

time: 69.2 us -> 58 us (0.84)
  Pallas kernels: 61.6 us -> 57.2 us
  other arithmetic: 3.45 us -> 0 us
  local copies, waits for them, and re-layouts: 3.22 us -> 0 us
    pallas_call x1, Pallas kernels: 61.6 us -> 55.7 us  [local(): pl.pallas_call(functools.partial(kernel, nlat, nlon), out_shape=(jax.Shap...]
    unnamed x12 -> x0, local copies, waits for them, and re-layouts: 2.5 us -> none
    reshape x2 -> x0, other arithmetic: 2.12 us -> none  [the longest x1 1.06 us: local(): one.astype(f32).reshape(shape)]
    pallas_call x0 -> x1, Pallas kernels: none -> 1.47 us  [local(): pl.pallas_call(widen, out_shape=(jax.ShapeDtypeStruct((ROWS * COLS, CH),...]
    select_n x1 -> x0, other arithmetic: 0.84 us -> none  [tap_table(): masked = jnp.where(keep[:, None, :, None], basis.astype(jnp.float32), 0.0)]
where the time goes in v2:
time: 58 us; the launch traced here: 57.8 us
  Pallas kernels  57.2 us (99%)
  between operations  0.64 us (1%)
    pallas_call x1, Pallas kernels, local(): pl.pallas_call(functools.partial(kernel, nlat, nlon), out_shape=(jax.Shap...  55.7 us
    pallas_call x1, Pallas kernels, local(): pl.pallas_call(widen, out_shape=(jax.ShapeDtypeStruct((ROWS * COLS, CH),...  1.47 us

profile of v2, /device:TPU:1, one launch (start us, length us, event | category | flops | bytes accessed | tf_op | source)
XLA Modules:
  0.0 57.8 jit_solution(9620818351686223873)
XLA Ops:
  0.6 55.7 %shard_map.85 = (f32[256,256]{1,0:T(8,128)S(1)}, bf16[1024,256]{1,0:T(8,128)(2,1)S(1)}, bf16[1024,256]{1,0:T(8,128)(2,1)S(1)}) custom-call(bf16[8,32,256]{2,1,0:T(8,128)(2,1)} %grid_ref.1, bf16[51,4,128]{2,1,0:T(4,128)(2,1)} %bitcast.5, s32[1,128]{1,0:T(1,128)} %bitcast.6, bf16[4,256,256]{2,1,0:T(8,128)(2,1)} %w1_ref.1, bf16[4,256,256]{2,1,0:T(8,128)(2,1)} %w2_ref.1, ...), custom_call_target="tpu_custom_call" | custom-call | tf_op jit(solution)/shard_map/pallas_call | solution.py:526
  56.4 1.5 %shard_map.86 = (f32[256,256]{1,0:T(8,128)}, f32[4,256,256]{2,1,0:T(8,128)}, f32[4,256,256]{2,1,0:T(8,128)}) custom-call(f32[256,256]{1,0:T(8,128)S(1)} %get-tuple-element.9.g_ref, bf16[1024,256]{1,0:T(8,128)(2,1)S(1)} %get-tuple-element.10.a_ref, bf16[1024,256]{1,0:T(8,128)(2,1)S(1)} %get-tuple-element.11.b_ref), custom_call_target="tpu_custom_call" | custom-call | tf_op jit(solution)/shard_map/pallas_call | solution.py:570

commit v3 on v2

--- a/solution.py
+++ b/solution.py
@@ -38,8 +38,20 @@
     lax.fori_loop(0, count, lambda i, c: (body(i), c)[1], 0, unroll=True)
 
 
-def ring_steps(count):
-    return sorted(range(1, count), key=lambda d: -min(d, count - d))
+def tree_sum(terms):
+    while len(terms) > 1:
+        pairs = [a + b for a, b in zip(terms[::2], terms[1::2])]
+        terms = pairs + terms[len(terms) // 2 * 2 :]
+    return terms[0]
+
+
+def ring_offsets(count):
+    return [0] + [d * s for d in range(1, count // 2) for s in (1, -1)] + [count // 2]
+
+
+def ring_groups(count, far):
+    cuts = [0, 5 * count // 16, far * count // 16, count]
+    return [(a, b - a) for a, b in zip(cuts, cuts[1:])]
 
 
 def plane_steps(nx, ny):
@@ -108,8 +120,7 @@
     w2_ref,
     cot_ref,
     gin_ref,
-    out1_ref,
-    out2_ref,
+    sums_ref,
     gext,
     cext,
     basis,
@@ -132,9 +143,10 @@
     crecv,
     xsend,
     xrecv,
-    zown,
+    xown,
+    zsend,
     zrecv,
-    zall,
+    out,
     local_sem,
     halo_send,
     halo_recv,
@@ -154,9 +166,9 @@
 ):
     nx, nz = nlat // 4, nlon // 2
     npl = nx * 4
-    xr = HALF // npl
-    zr = 2 * xr // nz
+    xr = 2 * HALF // npl
     zh = nz // 2
+    zr = xr // zh
     lat, lon = lax.axis_index("lat"), lax.axis_index("lon")
     core = lat % 2
     z = lon % nz
@@ -165,13 +177,14 @@
     def at(la, lo):
         return {"lat": la, "lon": lo}
 
-    plane, line = plane_steps(nx, 4), ring_steps(nz)
+    plane = plane_steps(nx, 4)
+    offsets, groups, last_groups = ring_offsets(nz), ring_groups(nz, 11), ring_groups(nz, 13)
 
     def plane_place(step):
         return ((me // 4 + step[0]) % nx) * 4 + (me + step[1]) % 4
 
-    def in_plane(q):
-        return at((q // 2) * 2 + core, (q % 2) * nz + z)
+    def in_plane(q, side=core):
+        return at((q // 2) * 2 + side, (q % 2) * nz + z)
 
     def in_z(q):
         return at(lat, (lon // nz) * nz + q)
@@ -225,7 +238,7 @@
 
     near = [device for device, *_ in neighbours]
     near += [sibling] + [in_plane(plane_place(step)) for step in plane]
-    near += [in_z((z + d) % nz) for d in (line if nz < 4 else (1, nz - 1))]
+    near += [in_z((z + d) % nz) for d in (1, nz - 1)]
     for device in near:
         signal(device, barrier)
     for copy in own:
@@ -347,7 +360,7 @@
 
     conv_own(hid, fband, store_z2)
     own[1].wait()
-    weight_grad(z2, cext[2 : 2 + ROWS, HALO : HALO + COLS, :].reshape(ROWS * COLS, CH), part2, 1)
+    weight_grad(z2, cext[2 : 2 + ROWS, HALO : HALO + COLS, :].reshape(ROWS * COLS, CH), part2, 0)
 
     def mix_back(cells, weight):
         total = dot_t(cells[:, :CH], weight[0])
@@ -366,103 +379,149 @@
             gown[(v - 1) * COLS : v * COLS, :] = grad_act[
                 v * MC + REACH : v * MC + REACH + COLS, :
             ].astype(jnp.bfloat16)
-    weight_grad(z1own, gown[...], part1, 0)
-
-    parts = (part1, part2)
-    outs = (out1_ref, out2_ref)
+    weight_grad(z1own, gown[...], part1, 1)
+
+    parts = (part2, part1)
     own_half = 2 * core
 
-    def plane_chunk(g, q):
-        k, row = q * xr // CH, (q * xr) % CH
-        row = pl.multiple_of(row, xr)
-        return parts[g][own_half + k, pl.ds(row, xr), :] + crecv[g, k, pl.ds(row, xr), :]
-
-    def plane_scatter(g):
-        await_bytes(crecv.at[g], core_recv.at[g])
-
-        for i, step in enumerate(plane):
-            q = plane_place(step)
-            xsend[g, i] = plane_chunk(g, q).astype(jnp.bfloat16)
+    def place_of(q):
+        offset = (q - z + nz + zh) % nz - zh
+        ahead = (offset > 0).astype(jnp.int32)
+        behind = (offset < 0).astype(jnp.int32)
+        far = (offset == -zh).astype(jnp.int32)
+        return 2 * offset * (ahead - behind) - ahead - far
+
+    places = [place_of(q) for q in range(nz)]
+
+    def plane_chunk(p, store):
+        row = (p // 2) * xr
+        k, row = row // CH, pl.multiple_of(row % CH, xr)
+        lanes = pl.ds(pl.multiple_of((p % 2) * 128, 128), 128)
+        for g in range(2):
+            rows = pl.ds(row, xr)
+            total = parts[g][own_half + k, rows, lanes] + crecv[g, k, rows, lanes]
+            for i in range(zh):
+                store(places[g * zh + i], total[i * zr : (i + 1) * zr, :])
+
+    def plane_send(slot, group):
+        first, count = groups[group]
+        some = pl.ds(first, count)
+        pltpu.make_async_remote_copy(
+            src_ref=xsend.at[slot, some],
+            dst_ref=xrecv.at[slot, some],
+            send_sem=x_send.at[group],
+            recv_sem=x_recv.at[group],
+            device_id=in_plane(plane_place(plane[slot])),
+            device_id_type=MESH,
+        ).start()
+
+    def plane_scatter():
+        for g in range(2):
+            await_bytes(crecv.at[g], core_recv.at[g])
+        for slot, step in enumerate(plane):
+
+            def store(place, value, slot=slot):
+                xsend[slot, place] = value.astype(jnp.bfloat16)
+
+            plane_chunk(plane_place(step), store)
+            plane_send(slot, len(groups) - 1)
+        for group in (1, 0):
+            for slot in range(len(plane)):
+                plane_send(slot, group)
+
+        def keep(place, value):
+            xown[place] = value
+
+        plane_chunk(me, keep)
+
+    def z_scatter(group):
+        first, count = groups[group]
+        await_bytes(xrecv.at[:, pl.ds(first, count)], x_recv.at[group])
+        terms = [xown[pl.ds(first, count)]]
+        terms += [xrecv[s, pl.ds(first, count)].astype(jnp.float32) for s in range(len(plane))]
+        zsend[pl.ds(first, count)] = tree_sum(terms)
+        for place in reversed(range(first, first + count)):
+            if place > 0:
+                pltpu.make_async_remote_copy(
+                    src_ref=zsend.at[place],
+                    dst_ref=zrecv.at[place - 1],
+                    send_sem=z_send.at[0],
+                    recv_sem=z_recv.at[0],
+                    device_id=in_z((z + nz + offsets[place]) % nz),
+                    device_id_type=MESH,
+                ).start()
+
+    def z_gather():
+        await_bytes(zrecv, z_recv.at[0])
+        total = tree_sum([zsend[0]] + [zrecv[place] for place in range(nz - 1)])
+        out[core, me, 0] = total.astype(jnp.bfloat16)
+        for place in reversed(range(1, nz)):
+            there = offsets.index(-offsets[place]) if 2 * offsets[place] < nz else place
+            group = sum(there >= first for first, _ in last_groups) - 1
             pltpu.make_async_remote_copy(
-                src_ref=xsend.at[g, i],
-                dst_ref=xrecv.at[g, i],
-                send_sem=x_send.at[g],
-                recv_sem=x_recv.at[g],
-                device_id=in_plane(q),
+                src_ref=out.at[core, me, 0],
+                dst_ref=out.at[core, me, there],
+                send_sem=zg_send.at[0],
+                recv_sem=zg_recv.at[group],
+                device_id=in_z((z + nz + offsets[place]) % nz),
                 device_id_type=MESH,
             ).start()
 
-    def z_scatter(g):
-        total = plane_chunk(g, me)
-        await_bytes(xrecv.at[g], x_recv.at[g])
-        for i in range(npl - 1):
-            total = total + xrecv[g, i].astype(jnp.float32)
-        for q in range(nz):
-            zown[g, q] = total[
-                (q % zh) * zr : (q % zh + 1) * zr, (q // zh) * 128 : (q // zh + 1) * 128
-            ]
-
-        for i, d in enumerate(line):
-            q = (z + d) % nz
-            pltpu.make_async_remote_copy(
-                src_ref=zown.at[g, q],
-                dst_ref=zrecv.at[g, i],
-                send_sem=z_send.at[g],
-                recv_sem=z_recv.at[g],
-                device_id=in_z(q),
-                device_id_type=MESH,
-            ).start()
-
-    def z_gather(g):
-        total = zown[g, z]
-        await_bytes(zrecv.at[g], z_recv.at[g])
-        for i in range(nz - 1):
-            total = total + zrecv[g, i]
-        zall[g, z] = total
-
-        for d in line:
-            pltpu.make_async_remote_copy(
-                src_ref=zall.at[g, z],
-                dst_ref=zall.at[g, z],
-                send_sem=zg_send.at[g],
-                recv_sem=zg_recv.at[g],
-                device_id=in_z((z + d) % nz),
-                device_id_type=MESH,
-            ).start()
-
-    def plane_gather(g):
-        await_bytes(zall.at[g, pl.ds(0, nz - 1)], zg_recv.at[g])
-        left = jnp.concatenate([zall[g, q] for q in range(zh)], axis=0)
-        right = jnp.concatenate([zall[g, zh + q] for q in range(zh)], axis=0)
-        rows = pl.ds(pl.multiple_of(core * HALF + me * xr, xr), xr)
-        out = outs[g]
-        out[rows, :] = jnp.concatenate([left, right], axis=1).astype(jnp.bfloat16)
-
-        for step in plane:
-            pltpu.make_async_remote_copy(
-                src_ref=out.at[rows],
-                dst_ref=out.at[rows],
-                send_sem=xg_send.at[g],
-                recv_sem=xg_recv.at[g],
-                device_id=in_plane(plane_place(step)),
-                device_id_type=MESH,
-            ).start()
-
-    def core_gather(g):
-        out = outs[g]
-        await_bytes(out.at[pl.ds(0, (npl - 1) * xr)], xg_recv.at[g])
-        rows = pl.ds(pl.multiple_of(core * HALF, HALF), HALF)
+    def gather(src, device, send, recv):
         pltpu.make_async_remote_copy(
-            src_ref=out.at[rows],
-            dst_ref=out.at[rows],
-            send_sem=f_send.at[g],
-            recv_sem=f_recv.at[g],
-            device_id=sibling,
+            src_ref=src,
+            dst_ref=src,
+            send_sem=send,
+            recv_sem=recv,
+            device_id=device,
             device_id_type=MESH,
         ).start()
 
-    plane_scatter(1)
-    plane_scatter(0)
+    def plane_gather(group):
+        first, count = last_groups[group]
+        own_chunk = 1 if first == 0 else 0
+        if count > own_chunk:
+            arrived = out.at[core, me, pl.ds(first + own_chunk, count - own_chunk)]
+            await_bytes(arrived, zg_recv.at[group])
+        some = out.at[core, me, pl.ds(first, count)]
+        for step in plane:
+            q = plane_place(step)
+            gather(some, in_plane(q), xg_send.at[group], xg_recv.at[group])
+            if group == 2:
+                gather(some, in_plane(q, 1 - core), f_send.at[group], f_recv.at[group])
+        if group == 2:
+            gather(some, sibling, f_send.at[group], f_recv.at[group])
+
+    def of_group(half, group, chips):
+        first, count = last_groups[group]
+        return out.at[half, pl.ds(0, chips), pl.ds(first, count)]
+
+    q_of = [(z + nz + offset) % nz for offset in offsets]
+    grad_of = [q // zh for q in q_of]
+    row_of = [pl.multiple_of((q % zh) * zr, zr) for q in q_of]
+
+    def emit(half, group):
+        first, count = last_groups[group]
+        for p in range(npl):
+            k, base = (p // 2) * xr // CH, (p // 2) * xr % CH
+            lanes = slice((p % 2) * 128, (p % 2 + 1) * 128)
+            for place in range(first, first + count):
+                rows = pl.ds(base + row_of[place], zr)
+                sums_ref[grad_of[place], 2 * half + k, rows, lanes] = out[half, p, place].astype(
+                    jnp.float32
+                )
+
+    def core_gather(group):
+        await_bytes(of_group(core, group, npl - 1), xg_recv.at[group])
+        if group < 2:
+            gather(of_group(core, group, npl), sibling, f_send.at[group], f_recv.at[group])
+        emit(core, group)
+
+    def finish(group):
+        await_bytes(of_group(core, group, npl), f_recv.at[group])
+        emit(1 - core, group)
+
+    plane_scatter()
 
     def store_back(i, k, value):
         zbuf[i * COLS : (i + 1) * COLS, k * CH : (k + 1) * CH] = value
@@ -471,35 +530,39 @@
     gin_ref[...] = mix_back(zbuf.at[pl.ds(0, ROWS * COLS)], w1)
 
     z_await(2)
-    z_scatter(1)
-    z_scatter(0)
-    z_gather(1)
-    z_gather(0)
-    plane_gather(1)
-    plane_gather(0)
+    for group in reversed(range(len(groups))):
+        z_scatter(group)
+    z_gather()
+    for group in range(3):
+        plane_gather(group)
+    core_gather(0)
     core_gather(1)
-    core_gather(0)
+    finish(0)
+    finish(1)
     for which, ext in enumerate((gext, cext)):
         await_bytes(ext.at[pl.ds(0, ROWS)], halo_send.at[which])
     for g in range(2):
         await_bytes(crecv.at[g], core_send.at[g])
-        await_bytes(xrecv.at[g], x_send.at[g])
-        await_bytes(zrecv.at[g], z_send.at[g])
-        await_bytes(zall.at[g, pl.ds(0, nz - 1)], zg_send.at[g])
-        await_bytes(outs[g].at[pl.ds(0, (npl - 1) * xr)], xg_send.at[g])
-    for g in range(2):
-        await_bytes(outs[g].at[pl.ds(0, HALF)], f_recv.at[g])
-        await_bytes(outs[g].at[pl.ds(0, HALF)], f_send.at[g])
-
-
-def widen(g_ref, a_ref, b_ref, g_out, a_out, b_out, a_buf, b_buf, g_sem, ab_sem):
+    await_bytes(zrecv, z_send.at[0])
+    await_bytes(out.at[core, me, pl.ds(0, nz - 1)], zg_send.at[0])
+    for group, (first, count) in enumerate(groups):
+        await_bytes(xrecv.at[:, pl.ds(first, count)], x_send.at[group])
+    for group in range(2):
+        await_bytes(of_group(core, group, npl - 1), xg_send.at[group])
+        await_bytes(of_group(core, group, npl), f_send.at[group])
+    core_gather(2)
+    finish(2)
+    await_bytes(of_group(core, 2, npl - 1), xg_send.at[2])
+    await_bytes(of_group(core, 2, npl), f_send.at[2])
+
+
+def write_out(g_ref, sums_ref, g_out, one_out, two_out, g_sem, sem):
     copies = [pltpu.make_async_copy(g_ref, g_out, g_sem)]
-    copies[0].start()
-    for n, (ref, buf, out) in enumerate(((a_ref, a_buf, a_out), (b_ref, b_buf, b_out))):
+    for n, out in enumerate((two_out, one_out)):
         for k in range(KB):
-            buf[k] = ref[k * CH : (k + 1) * CH, :].astype(jnp.float32)
-            copies.append(pltpu.make_async_copy(buf.at[k], out.at[k], ab_sem.at[n, k]))
-            copies[-1].start()
+            copies.append(pltpu.make_async_copy(sums_ref.at[n, k], out.at[k], sem.at[n, k]))
+    for copy in copies:
+        copy.start()
     for copy in copies:
         copy.wait()
 
@@ -507,8 +570,7 @@
 def local(grid_in, basis, widths, weight_one, weight_two, cotangent):
     nlat, nlon = lax.axis_size("lat"), lax.axis_size("lon")
     npl, nz = nlat, nlon // 2
-    xr = HALF // npl
-    zr = 2 * xr // nz
+    zr = 4 * HALF // (npl * nz)
     bf16, f32 = jnp.bfloat16, jnp.float32
     vmem, dma = pltpu.VMEM, pltpu.SemaphoreType.DMA
     hbm = pl.BlockSpec(memory_space=pltpu.HBM)
@@ -523,15 +585,14 @@
         pltpu.with_memory_space_constraint(x, pltpu.HBM)
         for x in (basis, widths.reshape(1, nlat_all))
     )
-    grad_in, one, two = pl.pallas_call(
+    grad_in, sums = pl.pallas_call(
         functools.partial(kernel, nlat, nlon),
         out_shape=(
             jax.ShapeDtypeStruct((ROWS * COLS, CH), f32),
-            jax.ShapeDtypeStruct((KB * CH, CH), bf16),
-            jax.ShapeDtypeStruct((KB * CH, CH), bf16),
+            jax.ShapeDtypeStruct((2, KB, CH, CH), f32),
         ),
         in_specs=[hbm] * 6,
-        out_specs=(on_chip, on_chip, on_chip),
+        out_specs=(on_chip, on_chip),
         scratch_shapes=[
             vmem((XR, XC, CH), bf16),
             vmem((XR, XC, CH), bf16),
@@ -553,14 +614,16 @@
             vmem((KB, CH, CH), f32),
             vmem((KB, CH, CH), f32),
             vmem((2, 2, CH, CH), f32),
-            vmem((2, npl - 1, xr, CH), bf16),
-            vmem((2, npl - 1, xr, CH), bf16),
-            vmem((2, nz, zr, 128), f32),
-            vmem((2, nz - 1, zr, 128), f32),
-            vmem((2, nz, zr, 128), f32),
+            vmem((npl - 1, nz, zr, 128), bf16),
+            vmem((npl - 1, nz, zr, 128), bf16),
+            vmem((nz, zr, 128), f32),
+            vmem((nz, zr, 128), f32),
+            vmem((nz - 1, zr, 128), f32),
+            vmem((2, npl, nz, zr, 128), bf16),
             dma((6,)),
         ]
-        + [dma((2,))] * 14
+        + [dma((2,))] * 4
+        + [dma((3,))] * 10
         + [pltpu.SemaphoreType.REGULAR((3,))],
         compiler_params=pltpu.CompilerParams(
             collective_id=0, has_side_effects=True, vmem_limit_bytes=48 * 1024 * 1024
@@ -568,13 +631,13 @@
     )(grid_in, basis, widths, weight_one, weight_two, cotangent)
     wide = jax.ShapeDtypeStruct(weight_one.shape, f32)
     grad_in, one, two = pl.pallas_call(
-        widen,
+        write_out,
         out_shape=(jax.ShapeDtypeStruct((ROWS * COLS, CH), f32), wide, wide),
-        in_specs=[on_chip] * 3,
+        in_specs=[on_chip] * 2,
         out_specs=(hbm, hbm, hbm),
-        scratch_shapes=[vmem(wide.shape, f32), vmem(wide.shape, f32), dma, dma((2, KB))],
+        scratch_shapes=[dma, dma((2, KB))],
         compiler_params=pltpu.CompilerParams(vmem_limit_bytes=16 * 1024 * 1024),
-    )(grad_in, one, two)
+    )(grad_in, sums)
     return grad_in.reshape(grid_in.shape), one, two
 
 

time: 58 us -> 56.4 us (0.972)
  Pallas kernels: 57.2 us -> 55.6 us
    pallas_call x1, Pallas kernels: 55.7 us -> 54.1 us  [local(): pl.pallas_call(functools.partial(kernel, nlat, nlon), out_shape=(jax.Shap...]
where the time goes in v3:
time: 56.4 us; the launch traced here: 56.2 us
  Pallas kernels  55.6 us (99%)
  between operations  0.64 us (1%)
    pallas_call x1, Pallas kernels, local(): pl.pallas_call(functools.partial(kernel, nlat, nlon), out_shape=(jax.Shap...  54.1 us
    pallas_call x1, Pallas kernels, local(): pl.pallas_call(write_out, out_shape=(jax.ShapeDtypeStruct((ROWS * COLS, C...  1.47 us

profile of v3, /device:TPU:1, one launch (start us, length us, event | category | flops | bytes accessed | tf_op | source)
XLA Modules:
  0.0 56.2 jit_solution(17039492570029856092)
XLA Ops:
  0.6 54.1 %shard_map.85 = (f32[256,256]{1,0:T(8,128)S(1)}, f32[2,4,256,256]{3,2,1,0:T(8,128)S(1)}) custom-call(bf16[8,32,256]{2,1,0:T(8,128)(2,1)} %grid_ref.1, bf16[51,4,128]{2,1,0:T(4,128)(2,1)} %bitcast.5, s32[1,128]{1,0:T(1,128)} %bitcast.6, bf16[4,256,256]{2,1,0:T(8,128)(2,1)} %w1_ref.1, bf16[4,256,256]{2,1,0:T(8,128)(2,1)} %w2_ref.1, bf16[8,32,256]{2,1,0:T(8,128)(2,1)} %cot_ref.1), custom_call_target="tpu_custom_call" | custom-call | tf_op jit(solution)/shard_map/pallas_call | solution.py:588
  54.8 1.5 %shard_map.86 = (f32[256,256]{1,0:T(8,128)}, f32[4,256,256]{2,1,0:T(8,128)}, f32[4,256,256]{2,1,0:T(8,128)}) custom-call(f32[256,256]{1,0:T(8,128)S(1)} %get-tuple-element.8.g_ref, f32[2,4,256,256]{3,2,1,0:T(8,128)S(1)} %get-tuple-element.9.sums_ref), custom_call_target="tpu_custom_call" | custom-call | tf_op jit(solution)/shard_map/pallas_call | solution.py:633

commit v4 on v3

--- a/solution.py
+++ b/solution.py
@@ -49,8 +49,8 @@
     return [0] + [d * s for d in range(1, count // 2) for s in (1, -1)] + [count // 2]
 
 
-def ring_groups(count, far):
-    cuts = [0, 5 * count // 16, far * count // 16, count]
+def ring_groups(count, near, far):
+    cuts = [0, near * count // 16, far * count // 16, count]
     return [(a, b - a) for a, b in zip(cuts, cuts[1:])]
 
 
@@ -140,6 +140,7 @@
     gown,
     part1,
     part2,
+    csend,
     crecv,
     xsend,
     xrecv,
@@ -178,7 +179,7 @@
         return {"lat": la, "lon": lo}
 
     plane = plane_steps(nx, 4)
-    offsets, groups, last_groups = ring_offsets(nz), ring_groups(nz, 11), ring_groups(nz, 13)
+    offsets, groups, last_groups = ring_offsets(nz), ring_groups(nz, 5, 11), ring_groups(nz, 7, 13)
 
     def plane_place(step):
         return ((me // 4 + step[0]) % nx) * 4 + (me + step[1]) % 4
@@ -259,12 +260,13 @@
         z_signal(0)
 
     for which, (src, ext) in enumerate(((grid_ref, gext), (cot_ref, cext))):
-        for device, rows, cols, row, count, col, width in neighbours:
+        for n, (device, rows, cols, row, count, col, width) in enumerate(neighbours):
+            beside_us = which + 2 * (n >= 6)
             pltpu.make_async_remote_copy(
                 src_ref=src.at[rows, cols],
                 dst_ref=ext.at[pl.ds(row, count), pl.ds(col, width)],
-                send_sem=halo_send.at[which],
-                recv_sem=halo_recv.at[which],
+                send_sem=halo_send.at[beside_us],
+                recv_sem=halo_recv.at[beside_us],
                 device_id=device,
                 device_id_type=MESH,
             ).start()
@@ -302,8 +304,10 @@
             return v + south * (2 * (XR - 2) + 1 - 2 * v)
         return v
 
-    def conv_wide(ext, band, keep_own):
-        for v in range(MR):
+    inner, outer = range(2, MR - 2), (0, 1, MR - 2, MR - 1)
+
+    def conv_wide(ext, band, keep_own, some):
+        for v in some:
             rows = jnp.concatenate([ext[slot(v + r)] for r in range(3)], axis=0)
             full = dot(band[v, :, :TAP], rows)
             mixed = full.astype(jnp.bfloat16)
@@ -317,6 +321,11 @@
                         k * MC + REACH : k * MC + REACH + COLS, :
                     ].astype(jnp.bfloat16)
 
+    def cells(buf, some):
+        if some is inner:
+            return buf[2 * MC : (MR - 2) * MC, :]
+        return jnp.concatenate([buf[: 2 * MC, :], buf[(MR - 2) * MC :, :]], axis=0)
+
     def conv_own(src, band, store):
         for i in range(ROWS):
             taps = jnp.concatenate(
@@ -327,27 +336,57 @@
             for k in range(KB):
                 store(i, k, mixed[k * COLS : (k + 1) * COLS, :])
 
+    def forward(some):
+        conv_wide(gext, fband, True, some)
+        act = dot(cells(zbuf, some), w1[...].reshape(KB * CH, CH))
+        tanh_val = jnp.tanh(GELU_C * (act + CUBIC * act * act * act))
+        slopes = 0.5 * (1.0 + tanh_val) + 0.5 * act * (1.0 - tanh_val * tanh_val) * GELU_C * (
+            1.0 + 3.0 * CUBIC * act * act
+        )
+        hidden = (0.5 * act * (1.0 + tanh_val)).astype(jnp.bfloat16)
+        for n, v in enumerate(some):
+            slope[v * MC : (v + 1) * MC, :] = slopes[n * MC : (n + 1) * MC, :]
+            hid[v, :MC, :] = hidden[n * MC : (n + 1) * MC, :]
+
+    def mix_back(total_cells, weight):
+        total = dot_t(total_cells[:, :CH], weight[0])
+        for k in range(1, KB):
+            total = total + dot_t(total_cells[:, k * CH : (k + 1) * CH], weight[k])
+        return total
+
+    def backward(some):
+        conv_wide(cext, aband, False, some)
+        grad_act = mix_back(cells(zbuf, some), w2) * cells(slope, some)
+        for n, v in enumerate(some):
+            gact[v, :MC, :] = grad_act[n * MC : (n + 1) * MC, :].astype(jnp.bfloat16)
+            if 1 <= v <= ROWS:
+                gown[(v - 1) * COLS : v * COLS, :] = grad_act[
+                    n * MC + REACH : n * MC + REACH + COLS, :
+                ].astype(jnp.bfloat16)
+
     own[0].wait()
-    await_bytes(gext.at[pl.ds(0, ROWS)], halo_recv.at[0])
+    await_bytes(gext.at[pl.ds(0, ROWS), pl.ds(0, 2 * HALO)], halo_recv.at[2])
     z_await(0)
-    conv_wide(gext, fband, True)
     own[2].wait()
-    act = dot(zbuf[...], w1[...].reshape(KB * CH, CH))
-    tanh_val = jnp.tanh(GELU_C * (act + CUBIC * act * act * act))
-    slope[...] = 0.5 * (1.0 + tanh_val) + 0.5 * act * (1.0 - tanh_val * tanh_val) * GELU_C * (
-        1.0 + 3.0 * CUBIC * act * act
-    )
-    hidden = (0.5 * act * (1.0 + tanh_val)).astype(jnp.bfloat16)
-    for v in range(MR):
-        hid[v, :MC, :] = hidden[v * MC : (v + 1) * MC, :]
+    forward(inner)
+    own[1].wait()
+    await_bytes(cext.at[pl.ds(0, ROWS), pl.ds(0, 2 * HALO)], halo_recv.at[3])
+    own[3].wait()
+    backward(inner)
+    await_bytes(gext.at[pl.ds(0, 4)], halo_recv.at[0])
+    z_await(1)
+    forward(outer)
 
     def weight_grad(cells, grad, part, g):
         for step in range(KB):
             k = (2 * (1 - core) + step) % KB
-            part[k] = t_dot(cells[k], grad)
-            if step < 2:
+            value = t_dot(cells[k], grad)
+            if step >= 2:
+                part[k] = value
+            else:
+                csend[g, step] = value.astype(jnp.bfloat16)
                 pltpu.make_async_remote_copy(
-                    src_ref=part.at[k],
+                    src_ref=csend.at[g, step],
                     dst_ref=crecv.at[g, step],
                     send_sem=core_send.at[g],
                     recv_sem=core_recv.at[g],
@@ -359,26 +398,9 @@
         z2[k, i * COLS : (i + 1) * COLS, :] = value
 
     conv_own(hid, fband, store_z2)
-    own[1].wait()
     weight_grad(z2, cext[2 : 2 + ROWS, HALO : HALO + COLS, :].reshape(ROWS * COLS, CH), part2, 0)
-
-    def mix_back(cells, weight):
-        total = dot_t(cells[:, :CH], weight[0])
-        for k in range(1, KB):
-            total = total + dot_t(cells[:, k * CH : (k + 1) * CH], weight[k])
-        return total
-
-    await_bytes(cext.at[pl.ds(0, ROWS)], halo_recv.at[1])
-    z_await(1)
-    conv_wide(cext, aband, False)
-    own[3].wait()
-    grad_act = mix_back(zbuf, w2) * slope[...]
-    for v in range(MR):
-        gact[v, :MC, :] = grad_act[v * MC : (v + 1) * MC, :].astype(jnp.bfloat16)
-        if 1 <= v <= ROWS:
-            gown[(v - 1) * COLS : v * COLS, :] = grad_act[
-                v * MC + REACH : v * MC + REACH + COLS, :
-            ].astype(jnp.bfloat16)
+    await_bytes(cext.at[pl.ds(0, 4)], halo_recv.at[1])
+    backward(outer)
     weight_grad(z1own, gown[...], part1, 1)
 
     parts = (part2, part1)
@@ -399,7 +421,7 @@
         lanes = pl.ds(pl.multiple_of((p % 2) * 128, 128), 128)
         for g in range(2):
             rows = pl.ds(row, xr)
-            total = parts[g][own_half + k, rows, lanes] + crecv[g, k, rows, lanes]
+            total = parts[g][own_half + k, rows, lanes] + crecv[g, k, rows, lanes].astype(jnp.float32)
             for i in range(zh):
                 store(places[g * zh + i], total[i * zr : (i + 1) * zr, :])
 
@@ -527,7 +549,7 @@
         zbuf[i * COLS : (i + 1) * COLS, k * CH : (k + 1) * CH] = value
 
     conv_own(gact, aband, store_back)
-    gin_ref[...] = mix_back(zbuf.at[pl.ds(0, ROWS * COLS)], w1)
+    gin_ref[...] = mix_back(zbuf[: ROWS * COLS, :], w1)
 
     z_await(2)
     for group in reversed(range(len(groups))):
@@ -540,7 +562,8 @@
     finish(0)
     finish(1)
     for which, ext in enumerate((gext, cext)):
-        await_bytes(ext.at[pl.ds(0, ROWS)], halo_send.at[which])
+        await_bytes(ext.at[pl.ds(0, 4)], halo_send.at[which])
+        await_bytes(ext.at[pl.ds(0, ROWS), pl.ds(0, 2 * HALO)], halo_send.at[which + 2])
     for g in range(2):
         await_bytes(crecv.at[g], core_send.at[g])
     await_bytes(zrecv, z_send.at[0])
@@ -613,7 +636,8 @@
             vmem((ROWS * COLS, CH), bf16),
             vmem((KB, CH, CH), f32),
             vmem((KB, CH, CH), f32),
-            vmem((2, 2, CH, CH), f32),
+            vmem((2, 2, CH, CH), bf16),
+            vmem((2, 2, CH, CH), bf16),
             vmem((npl - 1, nz, zr, 128), bf16),
             vmem((npl - 1, nz, zr, 128), bf16),
             vmem((nz, zr, 128), f32),
@@ -622,7 +646,8 @@
             vmem((2, npl, nz, zr, 128), bf16),
             dma((6,)),
         ]
-        + [dma((2,))] * 4
+        + [dma((4,))] * 2
+        + [dma((2,))] * 2
         + [dma((3,))] * 10
         + [pltpu.SemaphoreType.REGULAR((3,))],
         compiler_params=pltpu.CompilerParams(

time: 56.4 us -> 56 us (level)
  no operation moved by 1% of the time
where the time goes in v4:
time: 56 us; the launch traced here: 55.9 us
  Pallas kernels  55.3 us (99%)
  between operations  0.64 us (1%)
    pallas_call x1, Pallas kernels, local(): pl.pallas_call(functools.partial(kernel, nlat, nlon), out_shape=(jax.Shap...  53.8 us
    pallas_call x1, Pallas kernels, local(): pl.pallas_call(write_out, out_shape=(jax.ShapeDtypeStruct((ROWS * COLS, C...  1.47 us

profile of v4, /device:TPU:1, one launch (start us, length us, event | category | flops | bytes accessed | tf_op | source)
XLA Modules:
  0.0 55.9 jit_solution(4250495863056025049)
XLA Ops:
  0.6 53.8 %shard_map.85 = (f32[256,256]{1,0:T(8,128)S(1)}, f32[2,4,256,256]{3,2,1,0:T(8,128)S(1)}) custom-call(bf16[8,32,256]{2,1,0:T(8,128)(2,1)} %grid_ref.1, bf16[51,4,128]{2,1,0:T(4,128)(2,1)} %bitcast.5, s32[1,128]{1,0:T(1,128)} %bitcast.6, bf16[4,256,256]{2,1,0:T(8,128)(2,1)} %w1_ref.1, bf16[4,256,256]{2,1,0:T(8,128)(2,1)} %w2_ref.1, bf16[8,32,256]{2,1,0:T(8,128)(2,1)} %cot_ref.1), custom_call_target="tpu_custom_call" | custom-call | tf_op jit(solution)/shard_map/pallas_call | solution.py:611
  54.4 1.5 %shard_map.86 = (f32[256,256]{1,0:T(8,128)}, f32[4,256,256]{2,1,0:T(8,128)}, f32[4,256,256]{2,1,0:T(8,128)}) custom-call(f32[256,256]{1,0:T(8,128)S(1)} %get-tuple-element.8.g_ref, f32[2,4,256,256]{3,2,1,0:T(8,128)S(1)} %get-tuple-element.9.sums_ref), custom_call_target="tpu_custom_call" | custom-call | tf_op jit(solution)/shard_map/pallas_call | solution.py:658
